TPU v7x, 32 devices: a whole 2x2x4 slice. The times are simulated.
32 devices in a mesh: req: 16 (over z, x, core), tp: 2 (over y).
Axes of the slice: x: 2, y: 2, z: 4, core: 2. Of those that a mesh axis runs over, the one named last changes fastest.
Arguments:
- queries: bfloat16 [4096, 7168], P('req', 'tp'), may hold values from -200 to 200
- key_value: bfloat16 [2, 4096, 1024], P(None, 'req', 'tp'), may hold values from -8 to 8
- segment: int32 [4096], P('req'), may hold values from 0 to 7, never falling along the last dimension, each value on 1 to 1024 neighbouring positions
- residual: bfloat16 [4096, 7168], P('req', 'tp'), may hold values from -4 to 4
- out_weight: bfloat16 [7168, 7168], P('tp', 'req'), may hold values from -0.0625 to 0.0625
- head_gain: bfloat16 [7168], P('tp'), may hold values from 0.099609375 to 1.8984375
- vocab_weight: bfloat16 [7168, 64000], P('tp', 'req'), may hold values from -0.21875 to 0.21875
Outputs:
- hidden: bfloat16 [4096, 7168], P('req', 'tp')
- key_cache: bfloat16 [4096, 1024], P('req', 'tp')
- last_norm: float32 [8], replicated
- top_logit: float32 [8], replicated
Inputs may be any that keep to these rules, and one draw needn't show every extreme that they name: `segment`: ids never fall; each of the 8 requests has 1 to 1024 tokens, one has exactly 1024.
All inputs are finite; a program needn't handle non-finite values.
Results may differ from a plain program's by a relative error of at most 0.013.
Values may be sent and summed in bfloat16 or wider, within the bound.
A program may use at most 192 MiB of HBM per device.

v0:
```python
import jax
import jax.numpy as jnp
from jax import lax
from jax.sharding import PartitionSpec as P

D = 7168
HD = 128
GROUP = 7
REACH = 4


theta = 5000000.0
eps = 1e-05
masked_score = -1e30


def from_behind(value, axis, steps):
    count = lax.axis_size(axis)
    initial, last = (max(0, -steps), min(count, count - steps))
    return lax.ppermute(value, axis, [(source, source + steps) for source in range(initial, last)])


def rope_tables(positions, width):
    half_width = width // 2
    frequency = theta ** (-(jnp.arange(half_width, dtype=jnp.float32) * 2.0 / width))
    angles = positions[:, None] * frequency[None, :]
    return (jnp.cos(angles), jnp.sin(angles))


def rotate(values, cosine, sine_table):
    half_width = values.shape[-1] // 2
    first_half = values[..., :half_width]
    second_half = values[..., half_width:]
    table_shape = (cosine.shape[0],) + (1,) * (values.ndim - 2) + (half_width,)
    cosine = cosine.reshape(table_shape)
    sine_table = sine_table.reshape(table_shape)
    return jnp.concatenate(
        [
            first_half * cosine - second_half * sine_table,
            second_half * cosine + first_half * sine_table,
        ],
        axis=-1,
    )


def local(queries, key_value, segment, residual, out_weight, head_gain, vocab_weight):
    tok_rows = segment.shape[0]
    heads_kv = key_value.shape[2] // HD
    requests = lax.axis_size("req") // 2
    device = lax.axis_index("req")
    request_ids = jnp.arange(requests, dtype=jnp.int32)
    member = segment[:, None] == request_ids[None, :]
    counts = jnp.sum(member.astype(jnp.float32), axis=0)
    lengths = lax.psum(counts, "req")
    starts = jnp.cumsum(lengths) - lengths
    tok_index = (device * tok_rows).astype(jnp.float32) + jnp.arange(tok_rows, dtype=jnp.float32)
    own_start = jnp.sum(jnp.where(member, starts[None, :], 0.0), axis=1)
    positions = tok_index - own_start
    cosine, sine_table = rope_tables(positions, HD)
    rot_query = rotate(
        queries.astype(jnp.float32).reshape(tok_rows, heads_kv, GROUP, HD), cosine, sine_table
    ).astype(jnp.bfloat16)
    rot_key = rotate(
        key_value[0].astype(jnp.float32).reshape(tok_rows, heads_kv, HD), cosine, sine_table
    ).astype(jnp.bfloat16)
    key_cache = rot_key.reshape(tok_rows, heads_kv * HD)
    own_block = jnp.stack([key_cache, key_value[1]])
    blocks = [own_block]
    moving = own_block
    for offset in range(REACH):
        moving = from_behind(moving, "req", 1)
        blocks.insert(0, moving)
    window = jnp.concatenate(blocks, axis=1)
    span = window.shape[1]
    key_rows = window[0].reshape(span, heads_kv, HD)
    value_rows = window[1].reshape(span, heads_kv, HD)
    key_index = ((device - REACH) * tok_rows).astype(jnp.float32) + jnp.arange(
        span, dtype=jnp.float32
    )
    allowed = (key_index[None, :] >= own_start[:, None]) & (
        key_index[None, :] <= tok_index[:, None]
    )
    scale = HD ** (-0.5)
    scores_part = (
        jnp.einsum("qhgd,khd->hgqk", rot_query, key_rows, preferred_element_type=jnp.float32)
        * scale
    )
    scores = jnp.where(allowed[None, None], scores_part, masked_score)
    peak = jnp.max(scores, axis=3, keepdims=True)
    weights = jnp.exp(scores - peak)
    total = jnp.sum(weights, axis=3)
    context = jnp.einsum(
        "hgqk,khd->qhgd",
        weights.astype(jnp.bfloat16),
        value_rows,
        preferred_element_type=jnp.float32,
    )
    context = context / jnp.transpose(total, (2, 0, 1))[..., None]
    attended = context.astype(jnp.bfloat16).reshape(tok_rows, heads_kv * GROUP * HD)
    projected = jnp.dot(
        attended,
        lax.all_gather(out_weight, "req", axis=1, tiled=True),
        preferred_element_type=jnp.float32,
    )
    width_dev = residual.shape[1]
    summed = lax.psum(projected.astype(jnp.bfloat16), "tp").astype(jnp.float32)
    own_share = lax.dynamic_slice_in_dim(summed, lax.axis_index("tp") * width_dev, width_dev, 1)
    hidden = (residual.astype(jnp.float32) + own_share).astype(jnp.bfloat16)
    ends = starts + lengths - 1.0
    select = (tok_index[:, None] == ends[None, :]).astype(jnp.bfloat16)
    local_last = lax.dot_general(
        select, hidden, (((0,), (0,)), ((), ())), preferred_element_type=jnp.float32
    )
    last_state = lax.psum(local_last, "req")
    scaled = (last_state * head_gain.astype(jnp.float32)).astype(jnp.bfloat16)
    square_part = jnp.sum(last_state * last_state, axis=1)
    logit_part = jnp.dot(scaled, vocab_weight, preferred_element_type=jnp.float32)
    square_sum, raw_logits = (
        lax.psum(square_part.astype(jnp.bfloat16), "tp").astype(jnp.float32),
        lax.psum(logit_part.astype(jnp.bfloat16), "tp").astype(jnp.float32),
    )
    mean_square = square_sum / D
    last_norm = jnp.sqrt(mean_square)
    local_top = jnp.max(raw_logits * lax.rsqrt(mean_square + eps)[:, None], axis=1)
    top_logit = lax.pmax(local_top, "req")
    return (hidden, key_cache, last_norm, top_logit)


def solution(mesh):
    placed = (
        P("req", "tp"),
        P(None, "req", "tp"),
        P("req"),
        P("req", "tp"),
        P("tp", "req"),
        P("tp"),
        P("tp", "req"),
    )
    return jax.shard_map(
        local,
        mesh=mesh,
        in_specs=placed,
        out_specs=(P("req", "tp"), P("req", "tp"), P(), P()),
        check_vma=False,
    )
```

profile of v0, /device:TPU:0, one launch (start us, length us, event | category | flops | bytes accessed | tf_op | source)
XLA Modules:
  0.0 558.5 jit_solution(9607455848484133614)
XLA Ops:
  8.8 35.7 %psum.35 = f32[8]{0:T(128)S(1)} all-reduce(f32[8]{0:T(128)S(1)} %convert_reduce_fusion), channel_id=1, replica_groups=mesh['req'=16,'tp'=2] {'req'}, use_global_device_ids=true, to_apply=%region_1.0 | all-reduce | flops 8 | bytes 64 | tf_op jit(solution)/shard_map/psum | solution.py:54
  44.4 1.1 slice_convert_fusion
  46.6 1.3 collective-permute-start
  48.0 2.2 collective-permute-done
  50.2 15.4 %collective-permute-start.1 = (bf16[2,256,512]{1,2,0:T(8,128)(2,1)S(1)}, bf16[2,256,512]{1,2,0:T(8,128)(2,1)}, u32[]{:S(2)}, u32[]{:S(2)}) collective-permute-start(bf16[2,256,512]{1,2,0:T(8,128)(2,1)S(1)} %collective-permute-done), channel_id=1, source_target_pairs={{0,2},{2,4},{4,6},{6,8},{8,10},{10,12},{12,14},{14,16},{16,18},{18... | collective-permute-start | bytes 1572872 | tf_op jit(solution)/shard_map/ppermute | solution.py:20
  65.6 2.9 copy.38
  68.5 18.7 %collective-permute-start.2 = (bf16[2,256,512]{1,2,0:T(8,128)(2,1)}, bf16[2,256,512]{1,2,0:T(8,128)(2,1)}, u32[]{:S(2)}, u32[]{:S(2)}) collective-permute-start(bf16[2,256,512]{1,2,0:T(8,128)(2,1)} %collective-permute-done.1), channel_id=1, source_target_pairs={{0,2},{2,4},{4,6},{6,8},{8,10},{10,12},{12,14},{14,16},{16,18},{18... | collective-permute-start | bytes 1572872 | tf_op jit(solution)/shard_map/ppermute | solution.py:20
  88.3 21.1 %collective-permute-start.3 = (bf16[2,256,512]{1,2,0:T(8,128)(2,1)}, bf16[2,256,512]{1,2,0:T(8,128)(2,1)}, u32[]{:S(2)}, u32[]{:S(2)}) collective-permute-start(bf16[2,256,512]{1,2,0:T(8,128)(2,1)} %collective-permute-done.2), channel_id=1, source_target_pairs={{0,2},{2,4},{4,6},{6,8},{8,10},{10,12},{12,14},{14,16},{16,18},{18... | collective-permute-start | bytes 1572872 | tf_op jit(solution)/shard_map/ppermute | solution.py:20
  109.4 2.3 fusion.24
  111.9 3.8 copy.54
  115.7 2.5 copy.55
  118.2 4.4 subtract_convert_fusion
  126.1 16.1 %fusion.2 = (f32[4,7,256]{2,1,0:T(8,128)S(1)}, f32[4,1280,256,7]{2,1,3,0:T(8,128)}) fusion(pred[256,1280]{0,1:T(8,128)(4,1)S(1)} %compare_and_fusion, bf16[1280,4,128,1]{0,2,3,1:T(8,128)(2,1)S(1)} %bitcast.44, bf16[256,4,7,64]{3,0,2,1:T(8,128)(2,1)S(1)} %get-tuple-element.7, bf16[256,4,7,64]{3,0,2,1:T(8,128)(2,1)S(1)} %get-tuple-element.6), kind=kOutput, calls=%fused_computation.4 | convolution fusion | flops 2379998208 | bytes 40202240 | tf_op jit(solution)/shard_map/qhgd,khd->hgqk/dot_general | solution.py:85
  142.3 16.7 %fusion = f32[4,7,256]{2,1,0:T(8,128)S(1)} fusion(f32[4,1280,256,7]{2,1,3,0:T(8,128)} %get-tuple-element.23, f32[4,7,256]{2,1,0:T(8,128)S(1)} %get-tuple-element.22, pred[256,1280]{0,1:T(8,128)(4,1)S(1)} %compare_and_fusion), kind=kLoop, calls=%fused_computation.2 | loop fusion | flops 36692992 | bytes 37085184 | tf_op jit(solution)/shard_map/reduce_sum | solution.py:91
  159.0 18.1 %fusion.6 = bf16[256,4,7,128]{0,3,2,1:T(8,128)(2,1)} fusion(bf16[1280,4,128,1]{0,2,3,1:T(8,128)(2,1)S(1)} %bitcast.49, f32[4,1280,256,7]{2,1,3,0:T(8,128)} %get-tuple-element.23, f32[4,7,256]{2,1,0:T(8,128)S(1)} %get-tuple-element.22, pred[256,1280]{0,1:T(8,128)(4,1)S(1)} %compare_and_fusion, f32[256,4,7]{0,2,1:T(8,128)S(1)} %bitcast.50), kind=kOutput, calls=%fused_computation.10 | convolution fusion | flops 2387345408 | bytes 40230912 | tf_op jit(solution)/shard_map/hgqk,khd->qhgd/dot_general | solution.py:92
  177.0 105.6 %all-gather.2.cloned.1.call-done = bf16[3584,7168]{0,1:T(8,128)(2,1)} async-done(((bf16[3584,448]{0,1:T(8,128)(2,1)}), bf16[3584,7168]{0,1:T(8,128)(2,1)}) %all-gather.2.cloned.1.call-update) | async-done | bytes 51380240 | tf_op jit(solution)/shard_map/all_gather | solution.py:102
  282.7 22.5 %convolution_convert_fusion = bf16[256,7168]{1,0:T(8,128)(2,1)} fusion(bf16[256,3584]{0,1:T(8,128)(2,1)} %bitcast.52, bf16[3584,7168]{0,1:T(8,128)(2,1)} %all-gather.2.cloned.1.call-done), kind=kOutput, calls=%fused_computation.7 | convolution fusion | flops 13155172352 | bytes 56885248 | tf_op jit(solution)/shard_map/dot_general | solution.py:100
  305.2 101.9 %all-reduce.4.cloned.1.call-done = bf16[256,7168]{1,0:T(8,128)(2,1)} async-done(((bf16[256,7168]{1,0:T(8,128)(2,1)}), bf16[256,7168]{1,0:T(8,128)(2,1)}) %all-reduce.4.cloned.1.call-update) | async-done | bytes 3670032 | tf_op jit(solution)/shard_map/psum | solution.py:106
  407.1 2.5 add_convert_fusion
  409.6 1.2 fusion.13
  410.9 86.4 %all-reduce.6.cloned.1.call-done = f32[8,3584]{1,0:T(8,128)} async-done(((f32[8,3584]{1,0:T(8,128)}), f32[8,3584]{1,0:T(8,128)}) %all-reduce.6.cloned.1.call-update) | async-done | bytes 114704 | tf_op jit(solution)/shard_map/psum | solution.py:114
  497.3 13.0 %convolution_convert_fusion.1 = bf16[8,4000]{1,0:T(8,128)(2,1)S(1)} fusion(bf16[3584,4000]{0,1:T(8,128)(2,1)} %param.13, f32[8,3584]{1,0:T(8,128)} %all-reduce.6.cloned.1.call-done, f32[3584]{0:T(1024)S(1)} %convert_element_type.88), kind=kOutput, calls=%fused_computation.8 | convolution fusion | flops 229465344 | bytes 28865024 | tf_op jit(solution)/shard_map/dot_general | solution.py:117
  510.6 9.0 %all-reduce = (bf16[8]{0:T(256)(128)(2,1)S(1)}, bf16[8,4000]{1,0:T(8,128)(2,1)S(1)}) all-reduce(bf16[8]{0:T(256)(128)(2,1)S(1)} %multiply_reduce_fusion.1, bf16[8,4000]{1,0:T(8,128)(2,1)S(1)} %convolution_convert_fusion.1), channel_id=1, replica_groups=mesh['req'=16,'tp'=2] {'tp'}, use_global_device_ids=true, to_apply=%region_9.10 | all-reduce | flops 32008 | bytes 128032 | tf_op jit(solution)/shard_map/psum | solution.py:119
  521.1 30.9 %pmax.7 = f32[8]{0:T(128)} all-reduce(f32[8]{0:T(128)S(1)} %multiply_reduce_fusion), channel_id=1, replica_groups=mesh['req'=16,'tp'=2] {'req'}, use_global_device_ids=true, to_apply=%region_12.13 | all-reduce | flops 8 | bytes 64 | tf_op jit(solution)/shard_map/pmax | solution.py:125
  (51 shorter events, 9.2 us)
Async XLA Ops:
  7.2 38.9 %copy-start.6 = (s32[256]{0:T(256)S(1)}, s32[256]{0:T(256)}, u32[]{:S(2)}) copy-start(s32[256]{0:T(256)} %param.9) | copy-start | bytes 3076
  7.2 275.5 %all-gather.2.cloned.1.call-start = ((), (), s32[]{:S(2)}) async-start(), calls=%async_computation | async-start | bytes 54591488 | tf_op jit(solution)/shard_map/all_gather | solution.py:102
  7.9 399.2 %all-reduce.4.cloned.1.call-start = ((), (), s32[]{:S(2)}) async-start(), calls=%async_computation.1 | async-start | bytes 7340032 | tf_op jit(solution)/shard_map/psum | solution.py:106
  46.6 3.6 collective-permute-start
  50.2 59.2 %copy-start.3 = (bf16[2,256,512]{1,2,0:T(8,128)(2,1)}, bf16[2,256,512]{1,2,0:T(8,128)(2,1)S(1)}, u32[]{:S(2)}) copy-start(bf16[2,256,512]{1,2,0:T(8,128)(2,1)S(1)} %collective-permute-done) | copy-start | bytes 1572868
  50.2 18.3 %collective-permute-start.1 = (bf16[2,256,512]{1,2,0:T(8,128)(2,1)S(1)}, bf16[2,256,512]{1,2,0:T(8,128)(2,1)}, u32[]{:S(2)}, u32[]{:S(2)}) collective-permute-start(bf16[2,256,512]{1,2,0:T(8,128)(2,1)S(1)} %collective-permute-done), channel_id=1, source_target_pairs={{0,2},{2,4},{4,6},{6,8},{8,10},{10,12},{12,14},{14,16},{16,18},{18... | collective-permute-start | bytes 1572872 | tf_op jit(solution)/shard_map/ppermute | solution.py:20
  68.5 19.8 %collective-permute-start.2 = (bf16[2,256,512]{1,2,0:T(8,128)(2,1)}, bf16[2,256,512]{1,2,0:T(8,128)(2,1)}, u32[]{:S(2)}, u32[]{:S(2)}) collective-permute-start(bf16[2,256,512]{1,2,0:T(8,128)(2,1)} %collective-permute-done.1), channel_id=1, source_target_pairs={{0,2},{2,4},{4,6},{6,8},{8,10},{10,12},{12,14},{14,16},{16,18},{18... | collective-permute-start | bytes 1572872 | tf_op jit(solution)/shard_map/ppermute | solution.py:20
  88.3 34.3 %collective-permute-start.3 = (bf16[2,256,512]{1,2,0:T(8,128)(2,1)}, bf16[2,256,512]{1,2,0:T(8,128)(2,1)}, u32[]{:S(2)}, u32[]{:S(2)}) collective-permute-start(bf16[2,256,512]{1,2,0:T(8,128)(2,1)} %collective-permute-done.2), channel_id=1, source_target_pairs={{0,2},{2,4},{4,6},{6,8},{8,10},{10,12},{12,14},{14,16},{16,18},{18... | collective-permute-start | bytes 1572872 | tf_op jit(solution)/shard_map/ppermute | solution.py:20
  111.7 4.0 copy-start.1
  118.2 7.7 %copy-start.4 = (bf16[2,256,512]{1,2,0:T(8,128)(2,1)S(1)}, bf16[2,256,512]{1,2,0:T(8,128)(2,1)}, u32[]{:S(2)}) copy-start(bf16[2,256,512]{1,2,0:T(8,128)(2,1)} %copy-done.3) | copy-start | bytes 1572868
  305.2 192.2 %all-reduce.6.cloned.1.call-start = ((), (), s32[]{:S(2)}) async-start(), calls=%async_computation.2 | async-start | bytes 229376 | tf_op jit(solution)/shard_map/psum | solution.py:114
  305.2 105.7 %copy-start.5 = (bf16[3584]{0:T(1024)(128)(2,1)S(1)}, bf16[3584]{0:T(1024)(128)(2,1)}, u32[]{:S(2)}) copy-start(bf16[3584]{0:T(1024)(128)(2,1)} %param.12) | copy-start | bytes 21508
  409.6 100.8 %copy-start = (bf16[256,3584]{1,0:T(8,128)(2,1)}, bf16[256,3584]{1,0:T(8,128)(2,1)S(1)}, u32[]{:S(2)}) copy-start(bf16[256,3584]{1,0:T(8,128)(2,1)S(1)} %add_convert_fusion) | copy-start | bytes 5505028
  497.3 13.1 %copy-start.2 = (f32[8,3584]{1,0:T(8,128)S(1)}, f32[8,3584]{1,0:T(8,128)}, u32[]{:S(2)}) copy-start(f32[8,3584]{1,0:T(8,128)} %all-reduce.6.cloned.1.call-done) | copy-start | bytes 344068
Sparse Core Ops, SparseCore 0:
  9.6 273.0 all-gather.1
  305.3 101.8 all-reduce.3
  411.6 85.7 all-reduce.5
where the time goes:
time: 559 us
  waiting for transfers between devices  298 us (53%)
  blocking collectives  75.5 us (14%)
  matrix products  71 us (13%)
  starting transfers between devices  56.6 us (10%)
  other arithmetic  27.4 us (5%)
  local copies, waits for them, and re-layouts  16.3 us (3%)
  between operations  14 us (3%)
    all_gather x1, waiting for transfers between devices, local(): lax.all_gather(out_weight, 'req', axis=1, tiled=True)  106 us
    psum x1, waiting for transfers between devices, local(): summed = lax.psum(projected.astype(jnp.bfloat16), 'tp').astype(jnp.float32)  102 us
    psum x1, waiting for transfers between devices, local(): last_state = lax.psum(local_last, 'req')  86.4 us
    ppermute x4, starting transfers between devices, from_behind(): lax.ppermute(value, axis, [(source, source + steps) for source in range(i...  56.5 us
    psum x1, blocking collectives, local(): lengths = lax.psum(counts, 'req')  35.7 us
    pmax x1, blocking collectives, local(): top_logit = lax.pmax(local_top, 'req')  30.9 us
    dot_general x1, matrix products, local(): jnp.dot(attended, lax.all_gather(out_weight, 'req', axis=1, tiled=True),...  22.5 us
    dot_general x1, matrix products, local(): jnp.einsum('hgqk,khd->qhgd', weights.astype(jnp.bfloat16), value_rows, pr...  18.1 us
  transfers between devices with their start and end apart: 7, of which 5 were waited for; matrix products, arithmetic and copies ran while one was open for 13% of the time, Pallas kernels for 0%

commit v1 on v0

v1 whole, which is shorter than its diff:
```python
import math

import jax
import jax.numpy as jnp
from jax import lax
from jax.experimental import pallas as pl
from jax.experimental.pallas import tpu as pltpu
from jax.sharding import PartitionSpec as P

D = 7168
HD = 128
GROUP = 7
REACH = 4


theta = 5000000.0
eps = 1e-05
masked_score = -1e30


def from_behind(value, axis, steps):
    count = lax.axis_size(axis)
    initial, last = (max(0, -steps), min(count, count - steps))
    return lax.ppermute(value, axis, [(source, source + steps) for source in range(initial, last)])


def rope_tables(positions, width):
    half_width = width // 2
    frequency = theta ** (-(jnp.arange(half_width, dtype=jnp.float32) * 2.0 / width))
    angles = positions[:, None] * frequency[None, :]
    return (jnp.cos(angles), jnp.sin(angles))


def attend_kernel(seg_start, cosine, sine, queries, b4, b3, b2, b1, b0, attended, cache, bias, keys, values):
    rows = queries.shape[0]
    span = keys.shape[0]

    @pl.when(pl.program_id(0) == 0)
    def _():
        key_at = lax.broadcasted_iota(jnp.int32, (rows, span), 1)
        query_at = lax.broadcasted_iota(jnp.int32, (rows, span), 0) + (span - rows)
        keep = (key_at >= seg_start[...]) & (key_at <= query_at)
        bias[...] = jnp.where(keep, 0.0, masked_score)

    for at, block in enumerate((b4, b3, b2, b1, b0)):
        place = pl.ds(at * rows, rows)
        part = block[0].astype(jnp.float32)
        turned = part * cosine[place, :] + pltpu.roll(part, HD // 2, 1) * sine[place, :]
        keys[place, :] = turned.astype(jnp.bfloat16)
        values[place, :] = block[1]
    cache[...] = keys[pl.ds(span - rows, rows), :]
    own_cosine = cosine[pl.ds(span - rows, rows), :]
    own_sine = sine[pl.ds(span - rows, rows), :]
    rate = HD ** (-0.5) * math.log2(math.e)
    for head in range(GROUP):
        lanes = pl.ds(head * HD, HD)
        part = queries[:, lanes].astype(jnp.float32)
        turned = part * own_cosine + pltpu.roll(part, HD // 2, 1) * own_sine
        scores = lax.dot_general(
            turned.astype(jnp.bfloat16),
            keys[...],
            (((1,), (1,)), ((), ())),
            preferred_element_type=jnp.float32,
        )
        scores = scores + bias[...]
        peak = jnp.max(scores, axis=1, keepdims=True)
        weights = jnp.exp2((scores - peak) * rate)
        total = jnp.sum(weights, axis=1, keepdims=True)
        context = jnp.dot(
            weights.astype(jnp.bfloat16), values[...], preferred_element_type=jnp.float32
        )
        attended[:, lanes] = (context / total).astype(jnp.bfloat16)


def attend(seg_start, cosine, sine, queries, blocks):
    rows, width = queries.shape
    heads_kv = width // (GROUP * HD)
    span = cosine.shape[0]
    whole = lambda h: (0, 0)
    block_spec = pl.BlockSpec((2, rows, HD), lambda h: (0, 0, h))
    return pl.pallas_call(
        attend_kernel,
        grid=(heads_kv,),
        in_specs=[
            pl.BlockSpec((rows, 1), whole),
            pl.BlockSpec((span, HD), whole),
            pl.BlockSpec((span, HD), whole),
            pl.BlockSpec((rows, GROUP * HD), lambda h: (0, h)),
        ]
        + [block_spec] * (REACH + 1),
        out_specs=[
            pl.BlockSpec((rows, GROUP * HD), lambda h: (0, h)),
            pl.BlockSpec((rows, HD), lambda h: (0, h)),
        ],
        out_shape=[
            jax.ShapeDtypeStruct((rows, width), jnp.bfloat16),
            jax.ShapeDtypeStruct((rows, heads_kv * HD), jnp.bfloat16),
        ],
        scratch_shapes=[
            pltpu.VMEM((rows, span), jnp.float32),
            pltpu.VMEM((span, HD), jnp.bfloat16),
            pltpu.VMEM((span, HD), jnp.bfloat16),
        ],
        compiler_params=pltpu.CompilerParams(vmem_limit_bytes=40 * 2**20),
        cost_estimate=pl.CostEstimate(
            flops=4 * rows * span * width,
            bytes_accessed=4 * rows * width,
            transcendentals=rows * span * width // HD,
        ),
    )(seg_start, cosine, sine, queries, *blocks)


def project_by_weights(attended, out_weight, residual):
    projected = jnp.dot(
        attended,
        lax.all_gather(out_weight, "req", axis=1, tiled=True),
        preferred_element_type=jnp.float32,
    )
    width_dev = residual.shape[1]
    own_share = lax.psum_scatter(
        projected.astype(jnp.bfloat16), "tp", scatter_dimension=1, tiled=True
    ).astype(jnp.float32)
    return (residual.astype(jnp.float32) + own_share).astype(jnp.bfloat16)


def project_by_plane(attended, out_weight, residual):
    plane = 4
    depth = lax.axis_size("req") // plane
    groups = [[z * plane + i for i in range(plane)] for z in range(depth)]
    weights = lax.all_gather(out_weight, "req", axis_index_groups=groups)
    z = lax.axis_index("req") // plane
    y = lax.axis_index("tp")
    up, down = {}, {}
    forth = back = attended
    for step in range(1, depth):
        forth = from_behind(forth, "req", plane)
        back = from_behind(back, "req", -plane)
        up[step], down[step] = back, forth
    tokens = [
        attended,
        jnp.where(z % 2 == 0, up[1], down[1]),
        jnp.where(z < 2, up[2], down[2]),
        jnp.where(
            z == 0, up[3], jnp.where(z == 1, up[1], jnp.where(z == 2, down[1], down[3]))
        ),
    ]
    half = plane // 2
    kept_weights = lax.dynamic_slice_in_dim(weights, y * half, half, 0)
    sent_weights = lax.dynamic_slice_in_dim(weights, (1 - y) * half, half, 0)

    def product(rows, held):
        parts = [
            jnp.dot(rows, held[i], preferred_element_type=jnp.float32) for i in range(half)
        ]
        return jnp.concatenate(parts, axis=1)

    sums = []
    for rows in tokens:
        sent = product(rows, sent_weights).astype(jnp.bfloat16)
        kept = product(rows, kept_weights)
        came = lax.ppermute(sent, "tp", [(0, 1), (1, 0)])
        sums.append((kept + came.astype(jnp.float32)).astype(jnp.bfloat16))
    pieces = []
    for step in (0, 2, 1, 3):
        piece = jnp.where(y == 0, sums[step], sums[step ^ 2])
        moves = []
        for at in range(depth):
            for i in range(plane):
                for side in range(2):
                    to = at ^ step ^ (2 * side)
                    moves.append(((at * plane + i) * 2 + side, (to * plane + i) * 2 + at // 2))
        pieces.append((step, lax.ppermute(piece, ("req", "tp"), moves)))
    order = []
    for low in range(2):
        for side in range(2):
            step = z ^ (2 * y + low) ^ (2 * side)
            piece = pieces[0][1]
            for number, value in pieces[1:]:
                piece = jnp.where(step == number, value, piece)
            order.append(piece)
    return (residual.astype(jnp.float32) + jnp.concatenate(order, axis=1).astype(jnp.float32)).astype(
        jnp.bfloat16
    )


def local(queries, key_value, segment, residual, out_weight, head_gain, vocab_weight):
    tok_rows = segment.shape[0]
    requests = lax.axis_size("req") // 2
    device = lax.axis_index("req")
    request_ids = jnp.arange(requests, dtype=jnp.int32)
    segments = [from_behind(segment, "req", steps) for steps in range(REACH, 0, -1)] + [segment]
    blocks = [from_behind(key_value, "req", steps) for steps in range(REACH, 0, -1)] + [key_value]
    following = from_behind(segment, "req", -1)
    near = jnp.concatenate(segments)
    span = near.shape[0]
    at = jnp.arange(span, dtype=jnp.int32)
    real = at + (device - REACH) * tok_rows >= 0
    member = near[:, None] == request_ids[None, :]
    first = jnp.min(jnp.where(member & real[:, None], at[:, None], span), axis=0)
    start_at = jnp.sum(jnp.where(member, first[None, :], 0), axis=1)
    cosine, sine_table = rope_tables((at - start_at).astype(jnp.float32), HD)
    cosine = jnp.concatenate([cosine, cosine], axis=1)
    sine_table = jnp.concatenate([-sine_table, sine_table], axis=1)
    attended, key_cache = attend(
        start_at[span - tok_rows :, None], cosine, sine_table, queries, blocks
    )
    if lax.axis_size("req") == 16 and lax.axis_size("tp") == 2:
        hidden = project_by_plane(attended, out_weight, residual)
    else:
        hidden = project_by_weights(attended, out_weight, residual)
    after = jnp.concatenate([segment[1:], following[:1]])
    final = (device == lax.axis_size("req") - 1) & (jnp.arange(tok_rows) == tok_rows - 1)
    is_end = (segment != after) | final
    select = (is_end[:, None] & (segment[:, None] == request_ids[None, :])).astype(jnp.bfloat16)
    local_last = lax.dot_general(
        select, hidden, (((0,), (0,)), ((), ())), preferred_element_type=jnp.float32
    )
    last_state = lax.psum(local_last, "req")
    scaled = (last_state * head_gain.astype(jnp.float32)).astype(jnp.bfloat16)
    square_part = jnp.sum(last_state * last_state, axis=1)
    logit_part = jnp.dot(scaled, vocab_weight, preferred_element_type=jnp.float32)
    square_sum, raw_logits = (
        lax.psum(square_part.astype(jnp.bfloat16), "tp").astype(jnp.float32),
        lax.psum(logit_part.astype(jnp.bfloat16), "tp").astype(jnp.float32),
    )
    mean_square = square_sum / D
    last_norm = jnp.sqrt(mean_square)
    local_top = jnp.max(raw_logits * lax.rsqrt(mean_square + eps)[:, None], axis=1)
    top_logit = lax.pmax(local_top, "req")
    return (hidden, key_cache, last_norm, top_logit)


def solution(mesh):
    placed = (
        P("req", "tp"),
        P(None, "req", "tp"),
        P("req"),
        P("req", "tp"),
        P("tp", "req"),
        P("tp"),
        P("tp", "req"),
    )
    return jax.shard_map(
        local,
        mesh=mesh,
        in_specs=placed,
        out_specs=(P("req", "tp"), P("req", "tp"), P(), P()),
        check_vma=False,
    )
```

time: 559 us -> 538 us (0.962)
  local copies, waits for them, and re-layouts: 16.3 us -> 71.2 us
  matrix products: 71 us -> 30.7 us
  blocking collectives: 75.5 us -> 39.9 us
  Pallas kernels: 0 us -> 19.7 us
  waiting for transfers between devices: 298 us -> 285 us
  other arithmetic: 27.4 us -> 19 us
    ppermute x4 -> x15, waiting for transfers between devices: 2.97 us -> 139 us  [from_behind(): lax.ppermute(value, axis, [(source, source + steps) for source in range(i...]
    all_gather x1, waiting for transfers between devices: 106 us -> 0.01 us  [project_by_plane(): weights = lax.all_gather(out_weight, 'req', axis_index_groups=groups)]
    psum x1 -> x0, waiting for transfers between devices: 102 us -> none  [local(): summed = lax.psum(projected.astype(jnp.bfloat16), 'tp').astype(jnp.float32)]
    dot_general x3 -> x16, matrix products: 56.7 us -> 16.4 us  [product(): jnp.dot(rows, held[i], preferred_element_type=jnp.float32)]
    ppermute x0 -> x8, waiting for transfers between devices: none -> 39.8 us  [the longest x4 35.9 us: project_by_plane(): came = lax.ppermute(sent, 'tp', [(0, 1), (1, 0)])]
    psum x1 -> x0, blocking collectives: 35.7 us -> none  [local(): lengths = lax.psum(counts, 'req')]
    slice x2 -> x4, local copies, waits for them, and re-layouts: 2.48 us -> 35.7 us  [the longest x1 35.1 us: product(): held[i]]
    all_gather x0 -> x1, local copies, waits for them, and re-layouts: none -> 24.5 us  [project_by_plane(): weights = lax.all_gather(out_weight, 'req', axis_index_groups=groups)]
  transfers between devices with their start and end apart: 7 -> 25, of which waited for: 5 -> 11; matrix products, arithmetic and copies ran while one was open for 13% -> 4% of each run, Pallas kernels for 0% -> 4%
where the time goes in v1:
time: 538 us; the launch traced here: 536 us
  waiting for transfers between devices  285 us (53%)
  local copies, waits for them, and re-layouts  71.2 us (13%)
  starting transfers between devices  56.7 us (11%)
  blocking collectives  39.9 us (7%)
  matrix products  30.7 us (6%)
  Pallas kernels  19.7 us (4%)
  other arithmetic  19 us (4%)
  between operations  14.7 us (3%)
    ppermute x15, waiting for transfers between devices, from_behind(): lax.ppermute(value, axis, [(source, source + steps) for source in range(i...  139 us
    psum x1, waiting for transfers between devices, local(): last_state = lax.psum(local_last, 'req')  105 us
    ppermute x15, starting transfers between devices, from_behind(): lax.ppermute(value, axis, [(source, source + steps) for source in range(i...  44.9 us
    ppermute x4, waiting for transfers between devices, project_by_plane(): came = lax.ppermute(sent, 'tp', [(0, 1), (1, 0)])  35.9 us
    slice x1, local copies, waits for them, and re-layouts, product(): held[i]  35.1 us
    pmax x1, blocking collectives, local(): top_logit = lax.pmax(local_top, 'req')  30.9 us
    all_gather x1, local copies, waits for them, and re-layouts, project_by_plane(): weights = lax.all_gather(out_weight, 'req', axis_index_groups=groups)  24.5 us
    pallas_call x1, Pallas kernels, attend(): pl.pallas_call(attend_kernel, grid=(heads_kv,), in_specs=[pl.BlockSpec((r...  19.7 us
  transfers between devices with their start and end apart: 25, of which 11 were waited for; matrix products, arithmetic and copies ran while one was open for 4% of the time, Pallas kernels for 4%

profile of v1, /device:TPU:0, one launch (start us, length us, event | category | flops | bytes accessed | tf_op | source)
XLA Modules:
  0.0 536.4 jit_solution(6714248295552479879)
XLA Ops:
  10.3 4.4 collective-permute-start.2
  14.8 4.4 collective-permute-start.1
  31.2 3.8 collective-permute-start.7
  35.2 3.9 fusion.60
  41.4 8.2 %collective-permute-done.6.b2 = bf16[2,256,512]{2,1,0:T(8,128)(2,1)S(1)} collective-permute-done((bf16[2,256,512]{2,1,0:T(8,128)(2,1)S(1)}, bf16[2,256,512]{2,1,0:T(8,128)(2,1)S(1)}, u32[]{:S(2)}, u32[]{:S(2)}) %collective-permute-start.6) | collective-permute-done | bytes 524320 | tf_op jit(solution)/shard_map/ppermute | solution.py:24
  49.6 21.8 %collective-permute-done.5.b3 = bf16[2,256,512]{2,1,0:T(8,128)(2,1)S(1)} collective-permute-done((bf16[2,256,512]{2,1,0:T(8,128)(2,1)S(1)}, bf16[2,256,512]{2,1,0:T(8,128)(2,1)S(1)}, u32[]{:S(2)}, u32[]{:S(2)}) %collective-permute-start.5) | collective-permute-done | bytes 524320 | tf_op jit(solution)/shard_map/ppermute | solution.py:24
  71.4 19.7 %shard_map.102 = (bf16[256,3584]{1,0:T(8,128)(2,1)S(1)}, bf16[256,512]{1,0:T(8,128)(2,1)}) custom-call(s32[256,1]{1,0:T(8,128)S(1)} %copy.20.seg_start, f32[1280,128]{1,0:T(8,128)S(1)} %get-tuple-element.45.cosine, f32[1280,128]{1,0:T(8,128)S(1)} %get-tuple-element.46.sine, bf16[256,3584]{1,0:T(8,128)(2,1)S(1)} %copy-done, ...), custom_call_target="tpu_custom_call" | custom-call | flops 4697620480 | bytes 3670016 | tf_op jit(solution)/shard_map/pallas_call | solution.py:81
  95.0 36.9 %collective-permute-done.11 = bf16[256,3584]{1,0:T(8,128)(2,1)S(1)} collective-permute-done((bf16[256,3584]{1,0:T(8,128)(2,1)S(1)}, bf16[256,3584]{1,0:T(8,128)(2,1)S(1)}, u32[]{:S(2)}, u32[]{:S(2)}) %collective-permute-start.11) | collective-permute-done | bytes 1835040 | tf_op jit(solution)/shard_map/ppermute | solution.py:24
  131.8 4.5 collective-permute-start.12
  137.7 35.9 %collective-permute-done.12 = bf16[256,3584]{1,0:T(8,128)(2,1)S(1)} collective-permute-done((bf16[256,3584]{1,0:T(8,128)(2,1)S(1)}, bf16[256,3584]{1,0:T(8,128)(2,1)S(1)}, u32[]{:S(2)}, u32[]{:S(2)}) %collective-permute-start.12) | collective-permute-done | bytes 1835040 | tf_op jit(solution)/shard_map/ppermute | solution.py:24
  173.6 5.6 %collective-permute-start.13 = (bf16[256,3584]{1,0:T(8,128)(2,1)S(1)}, bf16[256,3584]{1,0:T(8,128)(2,1)}, u32[]{:S(2)}, u32[]{:S(2)}) collective-permute-start(bf16[256,3584]{1,0:T(8,128)(2,1)S(1)} %collective-permute-done.12), channel_id=1, source_target_pairs={{0,8},{2,10},{4,12},{6,14},{8,16},{10,18},{12,20},{14,22},{16,24},... | collective-permute-start | bytes 5505032 | tf_op jit(solution)/shard_map/ppermute | solution.py:24
  183.9 30.6 %collective-permute-done.13 = bf16[256,3584]{1,0:T(8,128)(2,1)} collective-permute-done((bf16[256,3584]{1,0:T(8,128)(2,1)S(1)}, bf16[256,3584]{1,0:T(8,128)(2,1)}, u32[]{:S(2)}, u32[]{:S(2)}) %collective-permute-start.13) | collective-permute-done | bytes 1835040 | tf_op jit(solution)/shard_map/ppermute | solution.py:24
  214.5 5.7 %collective-permute-done.10 = bf16[256,3584]{1,0:T(8,128)(2,1)} collective-permute-done((bf16[256,3584]{1,0:T(8,128)(2,1)}, bf16[256,3584]{1,0:T(8,128)(2,1)}, u32[]{:S(2)}, u32[]{:S(2)}) %collective-permute-start.10) | collective-permute-done | bytes 1835040 | tf_op jit(solution)/shard_map/ppermute | solution.py:24
  220.2 3.8 select_select_fusion
  223.9 24.5 %reshape.32 = bf16[4,3584,448]{1,0,2:T(4,128)(2,1)} reshape(bf16[14336,448]{0,1:T(8,128)(2,1)} %all-gather.3.cloned.1.call-done) | data formatting | bytes 25690112 | tf_op jit(solution)/shard_map/all_gather | solution.py:130
  248.4 35.1 %constant_dynamic-slice_fusion = (bf16[1,3584,448]{1,0,2:T(2,128)(2,1)}, bf16[1,3584,448]{1,0,2:T(2,128)(2,1)}, bf16[1,3584,448]{1,0,2:T(2,128)(2,1)}, bf16[1,3584,448]{1,0,2:T(2,128)(2,1)}) fusion(bf16[4,3584,448]{1,0,2:T(4,128)(2,1)} %reshape.32, s32[]{:T(128)S(6)} %select_n.160, s32[]{:T(128)S(6)} %select_n.161, s32[]{:T(128)S(6)} %add.64, s32[]{:T(128)S(6)} %add.63), kind=kLoop, calls=%fused_computation.92 | loop fusion | bytes 25690128 | tf_op jit(solution)/shard_map/slice | solution.py:153
  310.4 17.9 %collective-permute-done.14 = bf16[256,896]{0,1:T(8,128)(2,1)S(1)} collective-permute-done((bf16[256,896]{0,1:T(8,128)(2,1)S(1)}, bf16[256,896]{0,1:T(8,128)(2,1)S(1)}, u32[]{:S(2)}, u32[]{:S(2)}) %collective-permute-start.14) | collective-permute-done | bytes 458784 | tf_op jit(solution)/shard_map/ppermute | solution.py:161
  328.3 14.6 %collective-permute-done.15 = bf16[256,896]{0,1:T(8,128)(2,1)S(1)} collective-permute-done((bf16[256,896]{0,1:T(8,128)(2,1)S(1)}, bf16[256,896]{0,1:T(8,128)(2,1)S(1)}, u32[]{:S(2)}, u32[]{:S(2)}) %collective-permute-start.15) | collective-permute-done | bytes 458784 | tf_op jit(solution)/shard_map/ppermute | solution.py:161
  349.0 5.1 collective-permute-start.21
  361.1 3.9 collective-permute-done.20
  368.2 105.0 %all-reduce.3.cloned.1.call-done = f32[8,3584]{1,0:T(8,128)} async-done(((f32[8,3584]{1,0:T(8,128)}), f32[8,3584]{1,0:T(8,128)}) %all-reduce.3.cloned.1.call-update) | async-done | bytes 114704 | tf_op jit(solution)/shard_map/psum | solution.py:218
  473.2 13.0 %convolution_convert_fusion = bf16[8,4000]{1,0:T(8,128)(2,1)S(1)} fusion(bf16[3584,4000]{0,1:T(8,128)(2,1)} %param.13, f32[8,3584]{1,0:T(8,128)} %all-reduce.3.cloned.1.call-done, f32[3584]{0:T(1024)S(1)} %convert_element_type.77), kind=kOutput, calls=%fused_computation | convolution fusion | flops 229465344 | bytes 28865024 | tf_op jit(solution)/shard_map/dot_general | solution.py:221
  486.4 9.0 %all-reduce = (bf16[8]{0:T(256)(128)(2,1)S(1)}, bf16[8,4000]{1,0:T(8,128)(2,1)S(1)}) all-reduce(bf16[8]{0:T(256)(128)(2,1)S(1)} %multiply_reduce_fusion.1, bf16[8,4000]{1,0:T(8,128)(2,1)S(1)} %convolution_convert_fusion), channel_id=1, replica_groups=mesh['req'=16,'tp'=2] {'tp'}, use_global_device_ids=true, to_apply=%region_4.5 | all-reduce | flops 32008 | bytes 128032 | tf_op jit(solution)/shard_map/psum | solution.py:223
  498.7 30.9 %pmax.7 = f32[8]{0:T(128)} all-reduce(f32[8]{0:T(128)S(1)} %multiply_reduce_fusion), channel_id=1, replica_groups=mesh['req'=16,'tp'=2] {'req'}, use_global_device_ids=true, to_apply=%region_7.8 | all-reduce | flops 8 | bytes 64 | tf_op jit(solution)/shard_map/pmax | solution.py:229
  (134 shorter events, 73.8 us)
Async XLA Ops:
  7.2 216.8 %all-gather.3.cloned.1.call-start = ((), (), s32[]{:S(2)}) async-start(), calls=%async_computation.1 | async-start | bytes 16056320 | tf_op jit(solution)/shard_map/all_gather | solution.py:130
  7.9 465.3 %all-reduce.3.cloned.1.call-start = ((), (), s32[]{:S(2)}) async-start(), calls=%async_computation | async-start | bytes 229376 | tf_op jit(solution)/shard_map/psum | solution.py:218
  8.0 27.0 %collective-permute-start.3 = (s32[256]{0:T(256)S(1)}, s32[256]{0:T(256)S(1)}, u32[]{:S(2)}, u32[]{:S(2)}) collective-permute-start(s32[256]{0:T(256)S(1)} %copy-done.13), channel_id=1, source_target_pairs={{0,2},{2,4},{4,6},{6,8},{8,10},{10,12},{12,14},{14,16},{16,18},{18... | collective-permute-start | bytes 3080 | tf_op jit(solution)/shard_map/ppermute | solution.py:24
  10.3 20.8 %collective-permute-start.2 = (s32[256]{0:T(256)S(1)}, s32[256]{0:T(256)S(1)}, u32[]{:S(2)}, u32[]{:S(2)}) collective-permute-start(s32[256]{0:T(256)S(1)} %copy-done.13), channel_id=1, source_target_pairs={{0,4},{2,6},{4,8},{6,10},{8,12},{10,14},{12,16},{14,18},{16,20},{1... | collective-permute-start | bytes 3080 | tf_op jit(solution)/shard_map/ppermute | solution.py:24
  14.8 13.1 %collective-permute-start.1 = (s32[256]{0:T(256)S(1)}, s32[256]{0:T(256)S(1)}, u32[]{:S(2)}, u32[]{:S(2)}) collective-permute-start(s32[256]{0:T(256)S(1)} %copy-done.13), channel_id=1, source_target_pairs={{0,6},{2,8},{4,10},{6,12},{8,14},{10,16},{12,18},{14,20},{16,22},{... | collective-permute-start | bytes 3080 | tf_op jit(solution)/shard_map/ppermute | solution.py:24
  19.1 7.0 %collective-permute-start = (s32[256]{0:T(256)S(1)}, s32[256]{0:T(256)S(1)}, u32[]{:S(2)}, u32[]{:S(2)}) collective-permute-start(s32[256]{0:T(256)S(1)} %copy-done.13), channel_id=1, source_target_pairs={{0,8},{2,10},{4,12},{6,14},{8,16},{10,18},{12,20},{14,22},{16,24},... | collective-permute-start | bytes 3080 | tf_op jit(solution)/shard_map/ppermute | solution.py:24
  22.6 26.9 %collective-permute-start.6 = (bf16[2,256,512]{2,1,0:T(8,128)(2,1)S(1)}, bf16[2,256,512]{2,1,0:T(8,128)(2,1)S(1)}, u32[]{:S(2)}, u32[]{:S(2)}) collective-permute-start(bf16[2,256,512]{2,1,0:T(8,128)(2,1)S(1)} %copy-done.3), channel_id=1, source_target_pairs={{0,4},{2,6},{4,8},{6,10},{8,12},{10,14},{12,16},{14,18},{16,20},{1... | collective-permute-start | bytes 1572872 | tf_op jit(solution)/shard_map/ppermute | solution.py:24
  26.2 45.2 %collective-permute-start.5 = (bf16[2,256,512]{2,1,0:T(8,128)(2,1)S(1)}, bf16[2,256,512]{2,1,0:T(8,128)(2,1)S(1)}, u32[]{:S(2)}, u32[]{:S(2)}) collective-permute-start(bf16[2,256,512]{2,1,0:T(8,128)(2,1)S(1)} %copy-done.3), channel_id=1, source_target_pairs={{0,6},{2,8},{4,10},{6,12},{8,14},{10,16},{12,18},{14,20},{16,22},{... | collective-permute-start | bytes 1572872 | tf_op jit(solution)/shard_map/ppermute | solution.py:24
  27.9 43.5 %collective-permute-start.4 = (bf16[2,256,512]{2,1,0:T(8,128)(2,1)S(1)}, bf16[2,256,512]{2,1,0:T(8,128)(2,1)}, u32[]{:S(2)}, u32[]{:S(2)}) collective-permute-start(bf16[2,256,512]{2,1,0:T(8,128)(2,1)S(1)} %copy-done.3), channel_id=1, source_target_pairs={{0,8},{2,10},{4,12},{6,14},{8,16},{10,18},{12,20},{14,22},{16,24},... | collective-permute-start | bytes 1572872 | tf_op jit(solution)/shard_map/ppermute | solution.py:24
  31.2 40.2 %collective-permute-start.7 = (bf16[2,256,512]{2,1,0:T(8,128)(2,1)S(1)}, bf16[2,256,512]{2,1,0:T(8,128)(2,1)}, u32[]{:S(2)}, u32[]{:S(2)}) collective-permute-start(bf16[2,256,512]{2,1,0:T(8,128)(2,1)S(1)} %copy-done.3), channel_id=1, source_target_pairs={{0,2},{2,4},{4,6},{6,8},{8,10},{10,12},{12,14},{14,16},{16,18},{18... | collective-permute-start | bytes 1572872 | tf_op jit(solution)/shard_map/ppermute | solution.py:24
  91.1 40.8 %collective-permute-start.11 = (bf16[256,3584]{1,0:T(8,128)(2,1)S(1)}, bf16[256,3584]{1,0:T(8,128)(2,1)S(1)}, u32[]{:S(2)}, u32[]{:S(2)}) collective-permute-start(bf16[256,3584]{1,0:T(8,128)(2,1)S(1)} %get-tuple-element.6), channel_id=1, source_target_pairs={{0,8},{2,10},{4,12},{6,14},{8,16},{10,18},{12,20},{14,22},{16,24},... | collective-permute-start | bytes 5505032 | tf_op jit(solution)/shard_map/ppermute | solution.py:24
  93.7 42.7 %collective-permute-start.8 = (bf16[256,3584]{1,0:T(8,128)(2,1)S(1)}, bf16[256,3584]{1,0:T(8,128)(2,1)S(1)}, u32[]{:S(2)}, u32[]{:S(2)}) collective-permute-start(bf16[256,3584]{1,0:T(8,128)(2,1)S(1)} %get-tuple-element.6), channel_id=1, source_target_pairs={{8,0},{10,2},{12,4},{14,6},{16,8},{18,10},{20,12},{22,14},{24,16},... | collective-permute-start | bytes 5505032 | tf_op jit(solution)/shard_map/ppermute | solution.py:24
  131.8 41.7 %collective-permute-start.12 = (bf16[256,3584]{1,0:T(8,128)(2,1)S(1)}, bf16[256,3584]{1,0:T(8,128)(2,1)S(1)}, u32[]{:S(2)}, u32[]{:S(2)}) collective-permute-start(bf16[256,3584]{1,0:T(8,128)(2,1)S(1)} %collective-permute-done.11), channel_id=1, source_target_pairs={{0,8},{2,10},{4,12},{6,14},{8,16},{10,18},{12,20},{14,22},{16,24},... | collective-permute-start | bytes 5505032 | tf_op jit(solution)/shard_map/ppermute | solution.py:24
  136.4 42.9 %collective-permute-start.9 = (bf16[256,3584]{1,0:T(8,128)(2,1)S(1)}, bf16[256,3584]{1,0:T(8,128)(2,1)}, u32[]{:S(2)}, u32[]{:S(2)}) collective-permute-start(bf16[256,3584]{1,0:T(8,128)(2,1)S(1)} %collective-permute-done.8), channel_id=1, source_target_pairs={{8,0},{10,2},{12,4},{14,6},{16,8},{18,10},{20,12},{22,14},{24,16},... | collective-permute-start | bytes 5505032 | tf_op jit(solution)/shard_map/ppermute | solution.py:24
  173.6 40.9 %collective-permute-start.13 = (bf16[256,3584]{1,0:T(8,128)(2,1)S(1)}, bf16[256,3584]{1,0:T(8,128)(2,1)}, u32[]{:S(2)}, u32[]{:S(2)}) collective-permute-start(bf16[256,3584]{1,0:T(8,128)(2,1)S(1)} %collective-permute-done.12), channel_id=1, source_target_pairs={{0,8},{2,10},{4,12},{6,14},{8,16},{10,18},{12,20},{14,22},{16,24},... | collective-permute-start | bytes 5505032 | tf_op jit(solution)/shard_map/ppermute | solution.py:24
  179.2 41.0 %collective-permute-start.10 = (bf16[256,3584]{1,0:T(8,128)(2,1)}, bf16[256,3584]{1,0:T(8,128)(2,1)}, u32[]{:S(2)}, u32[]{:S(2)}) collective-permute-start(bf16[256,3584]{1,0:T(8,128)(2,1)} %collective-permute-done.9), channel_id=1, source_target_pairs={{8,0},{10,2},{12,4},{14,6},{16,8},{18,10},{20,12},{22,14},{24,16},... | collective-permute-start | bytes 5505032 | tf_op jit(solution)/shard_map/ppermute | solution.py:24
  305.0 39.4 %collective-permute-start.19 = (bf16[256,896]{0,1:T(8,128)(2,1)S(1)}, bf16[256,896]{0,1:T(8,128)(2,1)S(1)}, u32[]{:S(2)}, u32[]{:S(2)}) collective-permute-start(bf16[256,896]{0,1:T(8,128)(2,1)S(1)} %pad_maximum_fusion.5), channel_id=1, source_target_pairs={{0,1},{1,0},{2,3},{3,2},{4,5},{5,4},{6,7},{7,6},{8,9},{9,8},{10,11... | collective-permute-start | bytes 1376264 | tf_op jit(solution)/shard_map/ppermute | solution.py:161
  306.7 21.6 %collective-permute-start.14 = (bf16[256,896]{0,1:T(8,128)(2,1)S(1)}, bf16[256,896]{0,1:T(8,128)(2,1)S(1)}, u32[]{:S(2)}, u32[]{:S(2)}) collective-permute-start(bf16[256,896]{0,1:T(8,128)(2,1)S(1)} %pad_maximum_fusion.2), channel_id=1, source_target_pairs={{0,1},{1,0},{2,3},{3,2},{4,5},{5,4},{6,7},{7,6},{8,9},{9,8},{10,11... | collective-permute-start | bytes 1376264 | tf_op jit(solution)/shard_map/ppermute | solution.py:161
  307.2 35.7 %collective-permute-start.15 = (bf16[256,896]{0,1:T(8,128)(2,1)S(1)}, bf16[256,896]{0,1:T(8,128)(2,1)S(1)}, u32[]{:S(2)}, u32[]{:S(2)}) collective-permute-start(bf16[256,896]{0,1:T(8,128)(2,1)S(1)} %pad_maximum_fusion.3), channel_id=1, source_target_pairs={{0,1},{1,0},{2,3},{3,2},{4,5},{5,4},{6,7},{7,6},{8,9},{9,8},{10,11... | collective-permute-start | bytes 1376264 | tf_op jit(solution)/shard_map/ppermute | solution.py:161
  308.9 38.9 %collective-permute-start.18 = (bf16[256,896]{0,1:T(8,128)(2,1)S(1)}, bf16[256,896]{0,1:T(8,128)(2,1)S(1)}, u32[]{:S(2)}, u32[]{:S(2)}) collective-permute-start(bf16[256,896]{0,1:T(8,128)(2,1)S(1)} %pad_maximum_fusion.4), channel_id=1, source_target_pairs={{0,1},{1,0},{2,3},{3,2},{4,5},{5,4},{6,7},{7,6},{8,9},{9,8},{10,11... | collective-permute-start | bytes 1376264 | tf_op jit(solution)/shard_map/ppermute | solution.py:161
  343.9 17.2 %collective-permute-start.17 = (bf16[256,896]{0,1:T(8,128)(2,1)}, bf16[256,896]{0,1:T(8,128)(2,1)S(1)}, u32[]{:S(2)}, u32[]{:S(2)}) collective-permute-start(bf16[256,896]{0,1:T(8,128)(2,1)} %get-tuple-element.34), channel_id=1, source_target_pairs={{0,8},{1,24},{2,10},{3,26},{4,12},{5,28},{6,14},{7,30},{8,0},{9,16... | collective-permute-start | bytes 1376264 | tf_op jit(solution)/shard_map/ppermute | solution.py:172
  343.9 17.2 %collective-permute-start.16 = (bf16[256,896]{0,1:T(8,128)(2,1)S(1)}, bf16[256,896]{0,1:T(8,128)(2,1)S(1)}, u32[]{:S(2)}, u32[]{:S(2)}) collective-permute-start(bf16[256,896]{0,1:T(8,128)(2,1)S(1)} %get-tuple-element.35), channel_id=1, source_target_pairs={{0,24},{1,8},{2,26},{3,10},{4,28},{5,12},{6,30},{7,14},{8,16},{9,0... | collective-permute-start | bytes 1376264 | tf_op jit(solution)/shard_map/ppermute | solution.py:172
  349.0 12.1 %collective-permute-start.21 = (bf16[256,896]{0,1:T(8,128)(2,1)}, bf16[256,896]{0,1:T(8,128)(2,1)}, u32[]{:S(2)}, u32[]{:S(2)}) collective-permute-start(bf16[256,896]{0,1:T(8,128)(2,1)} %get-tuple-element.32), channel_id=1, source_target_pairs={{0,0},{1,16},{2,2},{3,18},{4,4},{5,20},{6,6},{7,22},{8,8},{9,24},{... | collective-permute-start | bytes 1376264 | tf_op jit(solution)/shard_map/ppermute | solution.py:172
  354.1 10.9 %collective-permute-start.20 = (bf16[256,896]{0,1:T(8,128)(2,1)}, bf16[256,896]{0,1:T(8,128)(2,1)}, u32[]{:S(2)}, u32[]{:S(2)}) collective-permute-start(bf16[256,896]{0,1:T(8,128)(2,1)} %get-tuple-element.33), channel_id=1, source_target_pairs={{0,16},{1,0},{2,18},{3,2},{4,20},{5,4},{6,22},{7,6},{8,24},{9,8},{... | collective-permute-start | bytes 1376264 | tf_op jit(solution)/shard_map/ppermute | solution.py:172
  (22 other events, 278.4 us)
Sparse Core Ops, SparseCore 0:
  9.6 104.7 all-gather.2
  368.3 104.8 all-reduce.2

commit v2 on v1

--- a/solution.py
+++ b/solution.py
@@ -1,3 +1,4 @@
+import functools
 import math
 
 import jax
@@ -69,7 +70,7 @@
         context = jnp.dot(
             weights.astype(jnp.bfloat16), values[...], preferred_element_type=jnp.float32
         )
-        attended[:, lanes] = (context / total).astype(jnp.bfloat16)
+        attended[0, :, lanes] = (context / total).astype(jnp.bfloat16)
 
 
 def attend(seg_start, cosine, sine, queries, blocks):
@@ -89,11 +90,11 @@
         ]
         + [block_spec] * (REACH + 1),
         out_specs=[
-            pl.BlockSpec((rows, GROUP * HD), lambda h: (0, h)),
+            pl.BlockSpec((1, rows, GROUP * HD), lambda h: (h, 0, 0)),
             pl.BlockSpec((rows, HD), lambda h: (0, h)),
         ],
         out_shape=[
-            jax.ShapeDtypeStruct((rows, width), jnp.bfloat16),
+            jax.ShapeDtypeStruct((heads_kv, rows, GROUP * HD), jnp.bfloat16),
             jax.ShapeDtypeStruct((rows, heads_kv * HD), jnp.bfloat16),
         ],
         scratch_shapes=[
@@ -111,6 +112,7 @@
 
 
 def project_by_weights(attended, out_weight, residual):
+    attended = jnp.swapaxes(attended, 0, 1).reshape(residual.shape[0], -1)
     projected = jnp.dot(
         attended,
         lax.all_gather(out_weight, "req", axis=1, tiled=True),
@@ -123,64 +125,382 @@
     return (residual.astype(jnp.float32) + own_share).astype(jnp.bfloat16)
 
 
+def plane_kernel(
+    attended, weights, share, held, blocks, acc, halves, halves_in, sums, pieces,
+    load_sems, z_send, z_recv, y_sems, c_send, c_recv,
+):
+    chunks, rows, depth = attended.shape
+    plane = held.shape[0]
+    half = plane // 2
+    count = blocks.shape[0]
+    me = lax.axis_index("req")
+    z, lane = me // plane, me % plane
+    y = lax.axis_index("tp")
+    other = 1 - y
+    at_home = y == z // 2
+
+    def at(to_z, to_y):
+        return {"req": to_z * plane + lane, "tp": to_y}
+
+    def load(j, c):
+        return pltpu.make_async_copy(
+            weights.at[j, pl.ds(c * depth, depth), :], held.at[j, c], load_sems.at[j, c]
+        )
+
+    def remote(source, landing, send, receive, target):
+        return pltpu.make_async_remote_copy(
+            src_ref=source,
+            dst_ref=landing,
+            send_sem=send,
+            recv_sem=receive,
+            device_id=target,
+            device_id_type=pl.DeviceIdType.MESH,
+        )
+
+    def along(source, origin, c, way):
+        return remote(
+            source,
+            blocks.at[origin, c],
+            z_send.at[way, origin, c],
+            z_recv.at[origin, c],
+            at(z + 1 - 2 * way, y),
+        )
+
+    def across(origin):
+        return remote(
+            halves.at[origin], halves_in.at[origin], y_sems.at[0, origin], y_sems.at[1, origin],
+            at(z, other),
+        )
+
+    def home(origin):
+        return remote(
+            sums.at[origin], pieces.at[z % 2, y], c_send.at[origin], c_recv.at[z % 2, y],
+            at(origin, z // 2),
+        )
+
+    def multiply(source, origin, c):
+        rows_here = source[...]
+
+        @pl.loop(0, plane)
+        def _(j):
+            acc[origin, j] += jnp.dot(rows_here, held[j, c], preferred_element_type=jnp.float32)
+
+    def send_half(origin):
+        for i in range(half):
+            halves[origin, i] = acc[origin, other * half + i].astype(jnp.bfloat16)
+        across(origin).start()
+
+    def send_home(origin):
+        across(origin).wait()
+        for i in range(half):
+            sums[origin, i] = (
+                acc[origin, y * half + i] + halves_in[origin, i].astype(jnp.float32)
+            ).astype(jnp.bfloat16)
+        stays = at_home & (origin == z)
+
+        @pl.when(stays)
+        def _():
+            pieces[z % 2, y] = sums[origin]
+
+        @pl.when(jnp.logical_not(stays))
+        def _():
+            home(origin).start()
+
+    for j in range(plane):
+        for c in range(chunks):
+            load(j, c).start()
+
+    barrier = pltpu.get_barrier_semaphore()
+
+    def greet(target):
+        pl.semaphore_signal(
+            barrier, inc=1, device_id=target, device_id_type=pl.DeviceIdType.MESH
+        )
+
+    has_up, has_down = z < count - 1, z > 0
+
+    @pl.when(has_up)
+    def _():
+        greet(at(z + 1, y))
+
+    @pl.when(has_down)
+    def _():
+        greet(at(z - 1, y))
+
+    greet(at(z, other))
+    for low in range(2):
+        for side in range(2):
+
+            @pl.when(jnp.logical_not((2 * y + low == z) & (side == y)))
+            def _():
+                greet(at(2 * y + low, side))
+
+    @pl.loop(0, count)
+    def _(origin):
+        @pl.loop(0, plane)
+        def _(j):
+            acc[origin, j] = jnp.zeros(acc.shape[2:], jnp.float32)
+
+    inner = jnp.where(has_up & has_down, 1, 0)
+    pl.semaphore_wait(barrier, 6 + inner - jnp.where(at_home, 1, 0))
+
+    @pl.loop(0, chunks)
+    def _(c):
+        @pl.when(has_up)
+        def _():
+            along(attended.at[c], z, c, 0).start()
+
+        @pl.when(has_down)
+        def _():
+            along(attended.at[c], z, c, 1).start()
+
+    @pl.loop(0, chunks)
+    def _(c):
+        for j in range(plane):
+            load(j, c).wait()
+        multiply(attended.at[c], z, c)
+
+    send_half(z)
+    for step in range(1, count):
+        below, above = z - step, z + step
+        from_below, from_above = below >= 0, above < count
+
+        @pl.loop(0, chunks)
+        def _(c):
+            @pl.when(from_below)
+            def _():
+                along(blocks.at[below, c], below, c, 0).wait_recv()
+
+                @pl.when(has_up)
+                def _():
+                    along(blocks.at[below, c], below, c, 0).start()
+
+            @pl.when(from_above)
+            def _():
+                along(blocks.at[above, c], above, c, 1).wait_recv()
+
+                @pl.when(has_down)
+                def _():
+                    along(blocks.at[above, c], above, c, 1).start()
+
+            @pl.when(from_below)
+            def _():
+                multiply(blocks.at[below, c], below, c)
+
+            @pl.when(from_above)
+            def _():
+                multiply(blocks.at[above, c], above, c)
+
+        @pl.when(from_below)
+        def _():
+            send_half(below)
+
+        @pl.when(from_above)
+        def _():
+            send_half(above)
+
+        if step == 1:
+            send_home(z)
+        else:
+
+            @pl.when(below + 1 >= 0)
+            def _():
+                send_home(below + 1)
+
+            @pl.when(above - 1 < count)
+            def _():
+                send_home(above - 1)
+
+    @pl.when(z == count - 1)
+    def _():
+        send_home(0)
+
+    @pl.when(z == 0)
+    def _():
+        send_home(count - 1)
+
+    for low in range(2):
+        for side in range(2):
+
+            @pl.when(jnp.logical_not((2 * y + low == z) & (side == y)))
+            def _():
+                remote(
+                    sums.at[0], pieces.at[low, side], c_send.at[0], c_recv.at[low, side],
+                    at(z, other),
+                ).wait_recv()
+
+            share[2 * low + side] = pieces[low, side]
+
+    for origin in range(count):
+
+        @pl.when(jnp.logical_not(at_home & (origin == z)))
+        def _():
+            home(origin).wait_send()
+
+        @pl.loop(0, chunks)
+        def _(c):
+            @pl.when(has_up & (origin <= z))
+            def _():
+                along(blocks.at[origin, c], origin, c, 0).wait_send()
+
+            @pl.when(has_down & (origin >= z))
+            def _():
+                along(blocks.at[origin, c], origin, c, 1).wait_send()
+
+
 def project_by_plane(attended, out_weight, residual):
     plane = 4
-    depth = lax.axis_size("req") // plane
-    groups = [[z * plane + i for i in range(plane)] for z in range(depth)]
+    count = lax.axis_size("req") // plane
+    groups = [[z * plane + i for i in range(plane)] for z in range(count)]
     weights = lax.all_gather(out_weight, "req", axis_index_groups=groups)
-    z = lax.axis_index("req") // plane
-    y = lax.axis_index("tp")
-    up, down = {}, {}
-    forth = back = attended
-    for step in range(1, depth):
-        forth = from_behind(forth, "req", plane)
-        back = from_behind(back, "req", -plane)
-        up[step], down[step] = back, forth
-    tokens = [
-        attended,
-        jnp.where(z % 2 == 0, up[1], down[1]),
-        jnp.where(z < 2, up[2], down[2]),
-        jnp.where(
-            z == 0, up[3], jnp.where(z == 1, up[1], jnp.where(z == 2, down[1], down[3]))
+    chunks, rows, depth = attended.shape
+    width = out_weight.shape[1]
+    half = plane // 2
+    bf16 = jnp.bfloat16
+    share = pl.pallas_call(
+        plane_kernel,
+        in_specs=[pl.BlockSpec(memory_space=pltpu.VMEM), pl.BlockSpec(memory_space=pl.ANY)],
+        out_specs=pl.BlockSpec(memory_space=pltpu.VMEM),
+        out_shape=jax.ShapeDtypeStruct((4, half, rows, width), bf16),
+        scratch_shapes=[
+            pltpu.VMEM((plane, chunks, depth, width), bf16),
+            pltpu.VMEM((count, chunks, rows, depth), bf16),
+            pltpu.VMEM((count, plane, rows, width), jnp.float32),
+            pltpu.VMEM((count, half, rows, width), bf16),
+            pltpu.VMEM((count, half, rows, width), bf16),
+            pltpu.VMEM((count, half, rows, width), bf16),
+            pltpu.VMEM((2, 2, half, rows, width), bf16),
+            pltpu.SemaphoreType.DMA((plane, chunks)),
+            pltpu.SemaphoreType.DMA((2, count, chunks)),
+            pltpu.SemaphoreType.DMA((count, chunks)),
+            pltpu.SemaphoreType.DMA((2, count)),
+            pltpu.SemaphoreType.DMA((count,)),
+            pltpu.SemaphoreType.DMA((2, 2)),
+        ],
+        compiler_params=pltpu.CompilerParams(
+            collective_id=1, has_side_effects=True, vmem_limit_bytes=58 * 2**20
         ),
-    ]
-    half = plane // 2
-    kept_weights = lax.dynamic_slice_in_dim(weights, y * half, half, 0)
-    sent_weights = lax.dynamic_slice_in_dim(weights, (1 - y) * half, half, 0)
-
-    def product(rows, held):
-        parts = [
-            jnp.dot(rows, held[i], preferred_element_type=jnp.float32) for i in range(half)
-        ]
-        return jnp.concatenate(parts, axis=1)
-
-    sums = []
-    for rows in tokens:
-        sent = product(rows, sent_weights).astype(jnp.bfloat16)
-        kept = product(rows, kept_weights)
-        came = lax.ppermute(sent, "tp", [(0, 1), (1, 0)])
-        sums.append((kept + came.astype(jnp.float32)).astype(jnp.bfloat16))
-    pieces = []
-    for step in (0, 2, 1, 3):
-        piece = jnp.where(y == 0, sums[step], sums[step ^ 2])
-        moves = []
-        for at in range(depth):
-            for i in range(plane):
-                for side in range(2):
-                    to = at ^ step ^ (2 * side)
-                    moves.append(((at * plane + i) * 2 + side, (to * plane + i) * 2 + at // 2))
-        pieces.append((step, lax.ppermute(piece, ("req", "tp"), moves)))
-    order = []
-    for low in range(2):
-        for side in range(2):
-            step = z ^ (2 * y + low) ^ (2 * side)
-            piece = pieces[0][1]
-            for number, value in pieces[1:]:
-                piece = jnp.where(step == number, value, piece)
-            order.append(piece)
-    return (residual.astype(jnp.float32) + jnp.concatenate(order, axis=1).astype(jnp.float32)).astype(
-        jnp.bfloat16
-    )
+        cost_estimate=pl.CostEstimate(
+            flops=2 * count * plane * rows * width * chunks * depth,
+            bytes_accessed=2 * plane * width * chunks * depth,
+            transcendentals=0,
+        ),
+    )(attended, weights)
+    own_share = share.reshape(2 * plane, rows, width).swapaxes(0, 1).reshape(residual.shape)
+    return (residual.astype(jnp.float32) + own_share.astype(jnp.float32)).astype(bf16)
+
+
+def partner(axis, step):
+    place = lax.axis_index(axis)
+    jump = 2**step
+    return {axis: place + jump * (1 - 2 * ((place // jump) % 2))}
+
+
+def exchange(source, landing, sems, place, target):
+    copy = pltpu.make_async_remote_copy(
+        src_ref=source,
+        dst_ref=landing,
+        send_sem=sems.at[0, place],
+        recv_sem=sems.at[1, place],
+        device_id=target,
+        device_id_type=pl.DeviceIdType.MESH,
+    )
+    copy.start()
+    copy.wait()
+
+
+def finish_kernel(
+    steps_req, steps_tp, select, hidden, gain, vocab, norm, top, weights, scaled,
+    states, states_in, parts, parts_in, tops, tops_in, load_sems, sems,
+):
+    chunks, chunk, words = weights.shape
+    targets = [partner("req", step) for step in range(steps_req)]
+    beside = [partner("tp", step) for step in range(steps_tp)]
+
+    def load(k):
+        return pltpu.make_async_copy(
+            vocab.at[pl.ds(k * chunk, chunk), :], weights.at[k], load_sems.at[k]
+        )
+
+    for k in range(chunks):
+        load(k).start()
+    barrier = pltpu.get_barrier_semaphore()
+    for target in targets + beside:
+        pl.semaphore_signal(
+            barrier, inc=1, device_id=target, device_id_type=pl.DeviceIdType.MESH
+        )
+    states[0] = lax.dot_general(
+        select[...], hidden[...], (((0,), (0,)), ((), ())), preferred_element_type=jnp.float32
+    )
+    pl.semaphore_wait(barrier, len(targets + beside))
+    for step, target in enumerate(targets):
+        exchange(states.at[step], states_in.at[step], sems, step, target)
+        states[step + 1] = states[step] + states_in[step]
+    last_state = states[steps_req]
+    scaled[...] = (last_state * gain[...].astype(jnp.float32)).astype(jnp.bfloat16)
+    edge = parts.shape[2] - 128
+    parts[0] = jnp.zeros(parts.shape[1:], jnp.float32)
+    parts[0, :, edge:] = jnp.broadcast_to(
+        jnp.sum(last_state * last_state, axis=1, keepdims=True), (parts.shape[1], 128)
+    )
+
+    @pl.loop(0, chunks)
+    def _(k):
+        load(k).wait()
+        columns = pl.ds(pl.multiple_of(k * chunk, chunk), chunk)
+        parts[0, :, :words] += jnp.dot(
+            scaled[:, columns], weights[k], preferred_element_type=jnp.float32
+        )
+
+    for step, target in enumerate(beside):
+        exchange(parts.at[step], parts_in.at[step], sems, steps_req + step, target)
+        parts[step + 1] = parts[step] + parts_in[step]
+    mean_square = parts[steps_tp, :, edge:] / D
+    norm[...] = jnp.sqrt(mean_square)
+    peak = jnp.max(parts[steps_tp, :, :words], axis=1, keepdims=True)
+    tops[0] = peak * lax.rsqrt(mean_square + eps)
+    for step, target in enumerate(targets):
+        exchange(tops.at[step], tops_in.at[step], sems, steps_req + steps_tp + step, target)
+        tops[step + 1] = jnp.maximum(tops[step], tops_in[step])
+    top[...] = tops[steps_req]
+
+
+def finish(select, hidden, head_gain, vocab_weight):
+    requests = select.shape[1]
+    depth, words = vocab_weight.shape
+    steps_req = lax.axis_size("req").bit_length() - 1
+    steps_tp = lax.axis_size("tp").bit_length() - 1
+    chunks = 7
+    wide = -(-words // 128) * 128 + 128
+    in_vmem = pl.BlockSpec(memory_space=pltpu.VMEM)
+    small = jax.ShapeDtypeStruct((requests, 128), jnp.float32)
+    norm, top = pl.pallas_call(
+        functools.partial(finish_kernel, steps_req, steps_tp),
+        in_specs=[in_vmem, in_vmem, in_vmem, pl.BlockSpec(memory_space=pl.ANY)],
+        out_specs=[in_vmem, in_vmem],
+        out_shape=[small, small],
+        scratch_shapes=[
+            pltpu.VMEM((chunks, depth // chunks, words), jnp.bfloat16),
+            pltpu.VMEM((requests, depth), jnp.bfloat16),
+            pltpu.VMEM((steps_req + 1, requests, depth), jnp.float32),
+            pltpu.VMEM((steps_req, requests, depth), jnp.float32),
+            pltpu.VMEM((steps_tp + 1, requests, wide), jnp.float32),
+            pltpu.VMEM((steps_tp, requests, wide), jnp.float32),
+            pltpu.VMEM((steps_req + 1, requests, 128), jnp.float32),
+            pltpu.VMEM((steps_req, requests, 128), jnp.float32),
+            pltpu.SemaphoreType.DMA((chunks,)),
+            pltpu.SemaphoreType.DMA((2, 2 * steps_req + steps_tp)),
+        ],
+        compiler_params=pltpu.CompilerParams(
+            collective_id=0, has_side_effects=True, vmem_limit_bytes=48 * 2**20
+        ),
+        cost_estimate=pl.CostEstimate(
+            flops=2 * requests * depth * words,
+            bytes_accessed=2 * depth * words,
+            transcendentals=0,
+        ),
+    )(select, hidden, head_gain[None, :], vocab_weight)
+    return norm[:, 0], top[:, 0]
 
 
 def local(queries, key_value, segment, residual, out_weight, head_gain, vocab_weight):
@@ -212,21 +532,7 @@
     final = (device == lax.axis_size("req") - 1) & (jnp.arange(tok_rows) == tok_rows - 1)
     is_end = (segment != after) | final
     select = (is_end[:, None] & (segment[:, None] == request_ids[None, :])).astype(jnp.bfloat16)
-    local_last = lax.dot_general(
-        select, hidden, (((0,), (0,)), ((), ())), preferred_element_type=jnp.float32
-    )
-    last_state = lax.psum(local_last, "req")
-    scaled = (last_state * head_gain.astype(jnp.float32)).astype(jnp.bfloat16)
-    square_part = jnp.sum(last_state * last_state, axis=1)
-    logit_part = jnp.dot(scaled, vocab_weight, preferred_element_type=jnp.float32)
-    square_sum, raw_logits = (
-        lax.psum(square_part.astype(jnp.bfloat16), "tp").astype(jnp.float32),
-        lax.psum(logit_part.astype(jnp.bfloat16), "tp").astype(jnp.float32),
-    )
-    mean_square = square_sum / D
-    last_norm = jnp.sqrt(mean_square)
-    local_top = jnp.max(raw_logits * lax.rsqrt(mean_square + eps)[:, None], axis=1)
-    top_logit = lax.pmax(local_top, "req")
+    last_norm, top_logit = finish(select, hidden, head_gain, vocab_weight)
     return (hidden, key_cache, last_norm, top_logit)
 
 

time: 538 us -> 391 us (0.73)
  waiting for transfers between devices: 285 us -> 28.9 us
  Pallas kernels: 19.7 us -> 230 us
  blocking collectives: 39.9 us -> 0 us
  matrix products: 30.7 us -> 0 us
  starting transfers between devices: 56.7 us -> 31.7 us
  other arithmetic: 19 us -> 13.6 us
    pallas_call x0 -> x2, Pallas kernels: none -> 211 us  [the longest x1 170 us: project_by_plane(): pl.pallas_call(plane_kernel, in_specs=[pl.BlockSpec(memory_space=pltpu.VM...]
    ppermute x15 -> x9, waiting for transfers between devices: 139 us -> 28.2 us  [from_behind(): lax.ppermute(value, axis, [(source, source + steps) for source in range(i...]
    psum x1 -> x0, waiting for transfers between devices: 105 us -> none  [local(): last_state = lax.psum(local_last, 'req')]
    ppermute x8 -> x0, waiting for transfers between devices: 39.8 us -> none  [the longest x4 35.9 us: project_by_plane(): came = lax.ppermute(sent, 'tp', [(0, 1), (1, 0)])]
    slice x1 -> x2, local copies, waits for them, and re-layouts: 35.1 us -> 1.25 us  [finish(): return (norm[:, 0], top[:, 0])]
    pmax x1 -> x0, blocking collectives: 30.9 us -> none  [local(): top_logit = lax.pmax(local_top, 'req')]
    dot_general x18 -> x0, matrix products: 30.7 us -> none  [the longest x16 16.4 us: product(): jnp.dot(rows, held[i], preferred_element_type=jnp.float32)]
    unnamed x52 -> x17, local copies, waits for them, and re-layouts: 10.9 us -> 38.4 us
  transfers between devices with their start and end apart: 25 -> 10, of which waited for: 11 -> 2; matrix products, arithmetic and copies ran while one was open for 4% -> 12% of each run, Pallas kernels for 4% -> 5%
where the time goes in v2:
time: 391 us; the launch traced here: 389 us
  Pallas kernels  230 us (59%)
  local copies, waits for them, and re-layouts  70.1 us (18%)
  starting transfers between devices  31.7 us (8%)
  waiting for transfers between devices  28.9 us (7%)
  between operations  14.2 us (4%)
  other arithmetic  13.6 us (3%)
    pallas_call x1, Pallas kernels, project_by_plane(): pl.pallas_call(plane_kernel, in_specs=[pl.BlockSpec(memory_space=pltpu.VM...  170 us
    pallas_call x1, Pallas kernels, finish(): pl.pallas_call(functools.partial(finish_kernel, steps_req, steps_tp), in_...  40.9 us
    unnamed x17, local copies, waits for them, and re-layouts  38.4 us
    ppermute x9, starting transfers between devices, from_behind(): lax.ppermute(value, axis, [(source, source + steps) for source in range(i...  31.7 us
    ppermute x9, waiting for transfers between devices, from_behind(): lax.ppermute(value, axis, [(source, source + steps) for source in range(i...  28.2 us
    pallas_call x1, Pallas kernels, attend(): pl.pallas_call(attend_kernel, grid=(heads_kv,), in_specs=[pl.BlockSpec((r...  19 us
    all_gather x1, local copies, waits for them, and re-layouts, project_by_plane(): weights = lax.all_gather(out_weight, 'req', axis_index_groups=groups)  17.8 us
    convert_element_type x2, local copies, waits for them, and re-layouts, project_by_plane(): own_share.astype(jnp.float32)  10.6 us
  transfers between devices with their start and end apart: 10, of which 2 were waited for; matrix products, arithmetic and copies ran while one was open for 12% of the time, Pallas kernels for 5%

profile of v2, /device:TPU:0, one launch (start us, length us, event | category | flops | bytes accessed | tf_op | source)
XLA Modules:
  0.0 388.9 jit_solution(8218978835203397239)
XLA Ops:
  7.9 1.3 collective-permute-start.8
  9.2 3.0 collective-permute-start.3
  12.2 4.8 %collective-permute-start.2 = (s32[256]{0:T(256)}, s32[256]{0:T(256)S(1)}, u32[]{:S(2)}, u32[]{:S(2)}) collective-permute-start(s32[256]{0:T(256)} %param.9), channel_id=1, source_target_pairs={{0,4},{2,6},{4,8},{6,10},{8,12},{10,14},{12,16},{14,18},{16,20},{1... | collective-permute-start | bytes 3080 | tf_op jit(solution)/shard_map/ppermute | solution.py:25
  17.1 3.9 %collective-permute-start.1 = (s32[256]{0:T(256)}, s32[256]{0:T(256)S(1)}, u32[]{:S(2)}, u32[]{:S(2)}) collective-permute-start(s32[256]{0:T(256)} %param.9), channel_id=1, source_target_pairs={{0,6},{2,8},{4,10},{6,12},{8,14},{10,16},{12,18},{14,20},{16,22},{... | collective-permute-start | bytes 3080 | tf_op jit(solution)/shard_map/ppermute | solution.py:25
  21.0 3.5 collective-permute-start
  24.5 0.8 slice.16
  26.0 37.1 %copy.29.vocab = bf16[3584,4000]{1,0:T(8,128)(2,1)} copy(bf16[3584,4000]{0,1:T(8,128)(2,1)} %param.13) | data formatting | bytes 57344000 | tf_op args[6]
  63.2 6.5 %collective-permute-start.6 = (bf16[2,256,512]{2,1,0:T(8,128)(2,1)S(1)}, bf16[2,256,512]{2,1,0:T(8,128)(2,1)S(1)}, u32[]{:S(2)}, u32[]{:S(2)}) collective-permute-start(bf16[2,256,512]{2,1,0:T(8,128)(2,1)S(1)} %copy-done.2), channel_id=1, source_target_pairs={{0,4},{2,6},{4,8},{6,10},{8,12},{10,14},{12,16},{14,18},{16,20},{1... | collective-permute-start | bytes 1572872 | tf_op jit(solution)/shard_map/ppermute | solution.py:25
  69.7 3.1 collective-permute-start.5
  72.8 2.5 collective-permute-start.4
  75.3 3.0 collective-permute-start.7
  79.1 3.9 fusion
  84.0 2.1 pad_maximum_fusion
  86.1 7.1 %collective-permute-done.6.b2 = bf16[2,256,512]{2,1,0:T(8,128)(2,1)S(1)} collective-permute-done((bf16[2,256,512]{2,1,0:T(8,128)(2,1)S(1)}, bf16[2,256,512]{2,1,0:T(8,128)(2,1)S(1)}, u32[]{:S(2)}, u32[]{:S(2)}) %collective-permute-start.6) | collective-permute-done | bytes 524320 | tf_op jit(solution)/shard_map/ppermute | solution.py:25
  93.1 21.1 %collective-permute-done.5.b3 = bf16[2,256,512]{2,1,0:T(8,128)(2,1)} collective-permute-done((bf16[2,256,512]{2,1,0:T(8,128)(2,1)S(1)}, bf16[2,256,512]{2,1,0:T(8,128)(2,1)}, u32[]{:S(2)}, u32[]{:S(2)}) %collective-permute-start.5) | collective-permute-done | bytes 524320 | tf_op jit(solution)/shard_map/ppermute | solution.py:25
  114.2 19.0 %shard_map.102 = (bf16[4,256,896]{2,1,0:T(8,128)(2,1)S(1)}, bf16[256,512]{1,0:T(8,128)(2,1)}) custom-call(s32[256,1]{1,0:T(8,128)S(1)} %copy.24.seg_start, f32[1280,128]{1,0:T(8,128)S(1)} %get-tuple-element.15.cosine, f32[1280,128]{1,0:T(8,128)S(1)} %get-tuple-element.16.sine, bf16[256,3584]{1,0:T(8,128)(2,1)S(1)} %copy-done.1, ...), custom_call_target="tpu_custom_call" | custom-call | flops 4697620480 | bytes 3670016 | tf_op jit(solution)/shard_map/pallas_call | solution.py:82
  133.2 1.2 copy-done.3
  134.5 17.8 %copy.25 = bf16[14336,448]{1,0:T(8,128)(2,1)} copy(bf16[14336,448]{0,1:T(8,128)(2,1)} %all-gather.3.cloned.1.call-done) | data formatting | bytes 25690112 | tf_op jit(solution)/shard_map/all_gather | solution.py:355
  152.3 170.4 %shard_map.103 = bf16[4,2,256,448]{3,2,1,0:T(8,128)(2,1)} custom-call(bf16[4,256,896]{2,1,0:T(8,128)(2,1)} %copy-done.3, bf16[4,3584,448]{2,1,0:T(8,128)(2,1)} %bitcast.9), custom_call_target="tpu_custom_call" | custom-call | flops 13153337344 | bytes 12845056 | tf_op jit(solution)/shard_map/pallas_call | solution.py:360
  322.7 4.1 %bitcast_convert_fusion = f32[8,256,448]{2,1,0:T(8,128)} fusion(bf16[4,2,256,448]{3,2,1,0:T(8,128)(2,1)} %shard_map.103), kind=kLoop, calls=%fused_computation.1 | loop fusion | flops 917504 | bytes 5505024 | tf_op jit(solution)/shard_map/convert_element_type | solution.py:390
  326.8 5.3 %copy.26 = f32[8,256,448]{1,2,0:T(8,128)} copy(f32[8,256,448]{2,1,0:T(8,128)} %bitcast_convert_fusion) | data formatting | bytes 7340032 | tf_op jit(solution)/shard_map/convert_element_type | solution.py:390
  332.1 5.3 %copy.27 = f32[256,3584]{1,0:T(8,128)} copy(f32[256,3584]{0,1:T(8,128)} %bitcast.8) | data formatting | bytes 7340032 | tf_op jit(solution)/shard_map/convert_element_type | solution.py:390
  337.4 2.4 add_convert_fusion.hidden
  339.9 40.9 %shard_map.104 = (f32[8,128]{1,0:T(8,128)S(1)}, f32[8,128]{1,0:T(8,128)S(1)}) custom-call(bf16[256,8]{1,0:T(8,128)(2,1)S(1)} %fusion.2.select, bf16[256,3584]{1,0:T(8,128)(2,1)S(1)} %add_convert_fusion.hidden, bf16[1,3584]{1,0:T(2,128)(2,1)S(1)} %broadcast_in_dim.45.gain, bf16[3584,4000]{1,0:T(8,128)(2,1)} %copy.29.vocab), custom_call_target="tpu_custom_call" | custom-call | flops 229376000 | bytes 28672000 | tf_op jit(solution)/shard_map/pallas_call | solution.py:477
  (40 shorter events, 4.5 us)
Async XLA Ops:
  7.2 127.3 %all-gather.3.cloned.1.call-start = ((), (), s32[]{:S(2)}) async-start(), calls=%async_computation | async-start | bytes 16056320 | tf_op jit(solution)/shard_map/all_gather | solution.py:355
  7.9 67.4 %collective-permute-start.8 = (s32[256]{0:T(256)}, s32[256]{0:T(256)S(1)}, u32[]{:S(2)}, u32[]{:S(2)}) collective-permute-start(s32[256]{0:T(256)} %param.9), channel_id=1, source_target_pairs={{2,0},{4,2},{6,4},{8,6},{10,8},{12,10},{14,12},{16,14},{18,16},{20... | collective-permute-start | bytes 3080 | tf_op jit(solution)/shard_map/ppermute | solution.py:25
  9.2 69.6 %collective-permute-start.3 = (s32[256]{0:T(256)}, s32[256]{0:T(256)S(1)}, u32[]{:S(2)}, u32[]{:S(2)}) collective-permute-start(s32[256]{0:T(256)} %param.9), channel_id=1, source_target_pairs={{0,2},{2,4},{4,6},{6,8},{8,10},{10,12},{12,14},{14,16},{16,18},{18... | collective-permute-start | bytes 3080 | tf_op jit(solution)/shard_map/ppermute | solution.py:25
  12.2 60.6 %collective-permute-start.2 = (s32[256]{0:T(256)}, s32[256]{0:T(256)S(1)}, u32[]{:S(2)}, u32[]{:S(2)}) collective-permute-start(s32[256]{0:T(256)} %param.9), channel_id=1, source_target_pairs={{0,4},{2,6},{4,8},{6,10},{8,12},{10,14},{12,16},{14,18},{16,20},{1... | collective-permute-start | bytes 3080 | tf_op jit(solution)/shard_map/ppermute | solution.py:25
  17.1 52.6 %collective-permute-start.1 = (s32[256]{0:T(256)}, s32[256]{0:T(256)S(1)}, u32[]{:S(2)}, u32[]{:S(2)}) collective-permute-start(s32[256]{0:T(256)} %param.9), channel_id=1, source_target_pairs={{0,6},{2,8},{4,10},{6,12},{8,14},{10,16},{12,18},{14,20},{16,22},{... | collective-permute-start | bytes 3080 | tf_op jit(solution)/shard_map/ppermute | solution.py:25
  21.0 42.1 %collective-permute-start = (s32[256]{0:T(256)}, s32[256]{0:T(256)S(1)}, u32[]{:S(2)}, u32[]{:S(2)}) collective-permute-start(s32[256]{0:T(256)} %param.9), channel_id=1, source_target_pairs={{0,8},{2,10},{4,12},{6,14},{8,16},{10,18},{12,20},{14,22},{16,24},... | collective-permute-start | bytes 3080 | tf_op jit(solution)/shard_map/ppermute | solution.py:25
  26.0 37.1 %copy-start.2 = (bf16[2,256,512]{2,1,0:T(8,128)(2,1)S(1)}, bf16[2,256,512]{2,1,0:T(8,128)(2,1)}, u32[]{:S(2)}) copy-start(bf16[2,256,512]{2,1,0:T(8,128)(2,1)} %b0.1) | copy-start | bytes 1572868
  26.0 52.8 %copy-start.5 = (s32[256]{0:T(256)S(1)}, s32[256]{0:T(256)}, u32[]{:S(2)}) copy-start(s32[256]{0:T(256)} %param.9) | copy-start | bytes 3076
  63.1 51.1 %copy-start.1 = (bf16[256,3584]{1,0:T(8,128)(2,1)S(1)}, bf16[256,3584]{1,0:T(8,128)(2,1)}, u32[]{:S(2)}) copy-start(bf16[256,3584]{1,0:T(8,128)(2,1)} %queries.1) | copy-start | bytes 5505028
  63.2 30.0 %collective-permute-start.6 = (bf16[2,256,512]{2,1,0:T(8,128)(2,1)S(1)}, bf16[2,256,512]{2,1,0:T(8,128)(2,1)S(1)}, u32[]{:S(2)}, u32[]{:S(2)}) collective-permute-start(bf16[2,256,512]{2,1,0:T(8,128)(2,1)S(1)} %copy-done.2), channel_id=1, source_target_pairs={{0,4},{2,6},{4,8},{6,10},{8,12},{10,14},{12,16},{14,18},{16,20},{1... | collective-permute-start | bytes 1572872 | tf_op jit(solution)/shard_map/ppermute | solution.py:25
  69.7 44.5 %collective-permute-start.5 = (bf16[2,256,512]{2,1,0:T(8,128)(2,1)S(1)}, bf16[2,256,512]{2,1,0:T(8,128)(2,1)}, u32[]{:S(2)}, u32[]{:S(2)}) collective-permute-start(bf16[2,256,512]{2,1,0:T(8,128)(2,1)S(1)} %copy-done.2), channel_id=1, source_target_pairs={{0,6},{2,8},{4,10},{6,12},{8,14},{10,16},{12,18},{14,20},{16,22},{... | collective-permute-start | bytes 1572872 | tf_op jit(solution)/shard_map/ppermute | solution.py:25
  72.8 41.4 %collective-permute-start.4 = (bf16[2,256,512]{2,1,0:T(8,128)(2,1)S(1)}, bf16[2,256,512]{2,1,0:T(8,128)(2,1)}, u32[]{:S(2)}, u32[]{:S(2)}) collective-permute-start(bf16[2,256,512]{2,1,0:T(8,128)(2,1)S(1)} %copy-done.2), channel_id=1, source_target_pairs={{0,8},{2,10},{4,12},{6,14},{8,16},{10,18},{12,20},{14,22},{16,24},... | collective-permute-start | bytes 1572872 | tf_op jit(solution)/shard_map/ppermute | solution.py:25
  75.3 38.9 %collective-permute-start.7 = (bf16[2,256,512]{2,1,0:T(8,128)(2,1)S(1)}, bf16[2,256,512]{2,1,0:T(8,128)(2,1)}, u32[]{:S(2)}, u32[]{:S(2)}) collective-permute-start(bf16[2,256,512]{2,1,0:T(8,128)(2,1)S(1)} %copy-done.2), channel_id=1, source_target_pairs={{0,2},{2,4},{4,6},{6,8},{8,10},{10,12},{12,14},{14,16},{16,18},{18... | collective-permute-start | bytes 1572872 | tf_op jit(solution)/shard_map/ppermute | solution.py:25
  133.2 1.2 copy-start.3
  332.1 5.3 %copy-start.4 = (bf16[256,3584]{1,0:T(8,128)(2,1)S(1)}, bf16[256,3584]{1,0:T(8,128)(2,1)}, u32[]{:S(2)}) copy-start(bf16[256,3584]{1,0:T(8,128)(2,1)} %param.10) | copy-start | bytes 5505028
  339.9 40.9 %copy-start = (bf16[256,3584]{1,0:T(8,128)(2,1)}, bf16[256,3584]{1,0:T(8,128)(2,1)S(1)}, u32[]{:S(2)}) copy-start(bf16[256,3584]{1,0:T(8,128)(2,1)S(1)} %add_convert_fusion.hidden) | copy-start | bytes 5505028
Sparse Core Ops, SparseCore 0:
  9.6 104.2 all-gather.2

commit v3 on v2

--- a/solution.py
+++ b/solution.py
@@ -126,8 +126,10 @@
 
 
 def plane_kernel(
-    attended, weights, share, held, blocks, acc, halves, halves_in, sums, pieces,
-    load_sems, z_send, z_recv, y_sems, c_send, c_recv,
+    seg_start, cosine, sine, queries, key_value, out_weight, share, cache,
+    attended, bias, keys, values, kv_in,
+    held, blocks, acc, halves, halves_in, sums, pieces,
+    kv_sems, load_sems, w_send, w_recv, z_send, z_recv, y_sems, c_send, c_recv,
 ):
     chunks, rows, depth = attended.shape
     plane = held.shape[0]
@@ -136,15 +138,18 @@
     me = lax.axis_index("req")
     z, lane = me // plane, me % plane
     y = lax.axis_index("tp")
+    mate = lane + 1 - 2 * (lane % 2)
+    facing = (lane + half) % plane
+    last = lax.axis_size("req") - 1
     other = 1 - y
     at_home = y == z // 2
 
     def at(to_z, to_y):
         return {"req": to_z * plane + lane, "tp": to_y}
 
-    def load(j, c):
+    def load(c):
         return pltpu.make_async_copy(
-            weights.at[j, pl.ds(c * depth, depth), :], held.at[j, c], load_sems.at[j, c]
+            out_weight.at[pl.ds(c * depth, depth), :], held.at[lane, c], load_sems.at[c]
         )
 
     def remote(source, landing, send, receive, target):
@@ -166,6 +171,26 @@
             at(z + 1 - 2 * way, y),
         )
 
+    def earlier(steps, target):
+        return remote(
+            key_value, kv_in.at[steps - 1], kv_sems.at[0, steps - 1], kv_sems.at[1, steps - 1],
+            {"req": target},
+        )
+
+    def spread(kind, c):
+        j = facing if kind == 2 else lane
+        source = held.at[facing, c] if kind == 2 else out_weight.at[pl.ds(c * depth, depth), :]
+        target = facing if kind == 1 else mate
+        return remote(
+            source, held.at[j, c], w_send.at[kind, c], w_recv.at[j, c], {"req": z * plane + target}
+        )
+
+    def take(j, c):
+        remote(
+            held.at[j, c], held.at[j, c], w_send.at[0, c], w_recv.at[j, c],
+            {"req": z * plane + mate},
+        ).wait_recv()
+
     def across(origin):
         return remote(
             halves.at[origin], halves_in.at[origin], y_sems.at[0, origin], y_sems.at[1, origin],
@@ -206,9 +231,8 @@
         def _():
             home(origin).start()
 
-    for j in range(plane):
-        for c in range(chunks):
-            load(j, c).start()
+    for c in range(chunks):
+        load(c).start()
 
     barrier = pltpu.get_barrier_semaphore()
 
@@ -228,12 +252,40 @@
         greet(at(z - 1, y))
 
     greet(at(z, other))
+    greet({"req": z * plane + mate})
+    greet({"req": z * plane + facing})
+    for steps in range(1, REACH + 1):
+
+        @pl.when(me >= steps)
+        def _():
+            greet({"req": me - steps})
+
     for low in range(2):
         for side in range(2):
 
             @pl.when(jnp.logical_not((2 * y + low == z) & (side == y)))
             def _():
                 greet(at(2 * y + low, side))
+
+    inner = jnp.where(has_up & has_down, 1, 0)
+    behind = jnp.minimum(last - me, REACH)
+    pl.semaphore_wait(barrier, 8 + inner + behind - jnp.where(at_home, 1, 0))
+
+    for steps in range(1, REACH + 1):
+
+        @pl.when(me + steps <= last)
+        def _():
+            earlier(steps, me + steps).start()
+
+    for c in range(chunks):
+        spread(1, c).start()
+        spread(0, c).start()
+
+    span = keys.shape[0]
+    key_at = lax.broadcasted_iota(jnp.int32, (rows, span), 1)
+    query_at = lax.broadcasted_iota(jnp.int32, (rows, span), 0) + (span - rows)
+    keep = (key_at >= seg_start[...]) & (key_at <= query_at)
+    bias[...] = jnp.where(keep, 0.0, masked_score)
 
     @pl.loop(0, count)
     def _(origin):
@@ -241,11 +293,49 @@
         def _(j):
             acc[origin, j] = jnp.zeros(acc.shape[2:], jnp.float32)
 
-    inner = jnp.where(has_up & has_down, 1, 0)
-    pl.semaphore_wait(barrier, 6 + inner - jnp.where(at_home, 1, 0))
+    for steps in range(1, REACH + 1):
+
+        @pl.when(me < steps)
+        def _():
+            kv_in[steps - 1] = jnp.zeros(kv_in.shape[1:], jnp.bfloat16)
+
+        @pl.when(me >= steps)
+        def _():
+            earlier(steps, mate).wait_recv()
+
+    rate = HD ** (-0.5) * math.log2(math.e)
 
     @pl.loop(0, chunks)
     def _(c):
+        lanes_kv = pl.ds(pl.multiple_of(c * HD, HD), HD)
+        for number in range(REACH + 1):
+            place = pl.ds(number * rows, rows)
+            block = key_value if number == REACH else kv_in.at[REACH - 1 - number]
+            part = block[0, :, lanes_kv].astype(jnp.float32)
+            turned = part * cosine[place, :] + pltpu.roll(part, HD // 2, 1) * sine[place, :]
+            keys[place, :] = turned.astype(jnp.bfloat16)
+            values[place, :] = block[1, :, lanes_kv]
+        own = pl.ds(span - rows, rows)
+        cache[:, lanes_kv] = keys[own, :]
+        for head in range(GROUP):
+            lanes = pl.ds(pl.multiple_of(c * depth + head * HD, HD), HD)
+            part = queries[:, lanes].astype(jnp.float32)
+            turned = part * cosine[own, :] + pltpu.roll(part, HD // 2, 1) * sine[own, :]
+            scores = lax.dot_general(
+                turned.astype(jnp.bfloat16),
+                keys[...],
+                (((1,), (1,)), ((), ())),
+                preferred_element_type=jnp.float32,
+            )
+            scores = scores + bias[...]
+            peak = jnp.max(scores, axis=1, keepdims=True)
+            weights = jnp.exp2((scores - peak) * rate)
+            total = jnp.sum(weights, axis=1, keepdims=True)
+            context = jnp.dot(
+                weights.astype(jnp.bfloat16), values[...], preferred_element_type=jnp.float32
+            )
+            attended[c, :, pl.ds(head * HD, HD)] = (context / total).astype(jnp.bfloat16)
+
         @pl.when(has_up)
         def _():
             along(attended.at[c], z, c, 0).start()
@@ -256,8 +346,14 @@
 
     @pl.loop(0, chunks)
     def _(c):
-        for j in range(plane):
-            load(j, c).wait()
+        take(facing, c)
+        spread(2, c).start()
+
+    @pl.loop(0, chunks)
+    def _(c):
+        load(c).wait()
+        take(mate, c)
+        take((mate + half) % plane, c)
         multiply(attended.at[c], z, c)
 
     send_half(z)
@@ -331,6 +427,17 @@
 
             share[2 * low + side] = pieces[low, side]
 
+    for steps in range(1, REACH + 1):
+
+        @pl.when(me + steps <= last)
+        def _():
+            earlier(steps, me + steps).wait_send()
+
+    @pl.loop(0, chunks)
+    def _(c):
+        for kind in range(3):
+            spread(kind, c).wait_send()
+
     for origin in range(count):
 
         @pl.when(jnp.logical_not(at_home & (origin == z)))
@@ -348,21 +455,31 @@
                 along(blocks.at[origin, c], origin, c, 1).wait_send()
 
 
-def project_by_plane(attended, out_weight, residual):
+def attend_and_project(seg_start, cosine, sine, queries, key_value, out_weight, residual):
     plane = 4
     count = lax.axis_size("req") // plane
-    groups = [[z * plane + i for i in range(plane)] for z in range(count)]
-    weights = lax.all_gather(out_weight, "req", axis_index_groups=groups)
-    chunks, rows, depth = attended.shape
+    rows = queries.shape[0]
+    chunks = key_value.shape[2] // HD
+    depth = GROUP * HD
+    span = cosine.shape[0]
     width = out_weight.shape[1]
     half = plane // 2
     bf16 = jnp.bfloat16
-    share = pl.pallas_call(
+    in_vmem = pl.BlockSpec(memory_space=pltpu.VMEM)
+    share, key_cache = pl.pallas_call(
         plane_kernel,
-        in_specs=[pl.BlockSpec(memory_space=pltpu.VMEM), pl.BlockSpec(memory_space=pl.ANY)],
-        out_specs=pl.BlockSpec(memory_space=pltpu.VMEM),
-        out_shape=jax.ShapeDtypeStruct((4, half, rows, width), bf16),
+        in_specs=[in_vmem] * 5 + [pl.BlockSpec(memory_space=pl.ANY)],
+        out_specs=[in_vmem, in_vmem],
+        out_shape=[
+            jax.ShapeDtypeStruct((4, half, rows, width), bf16),
+            jax.ShapeDtypeStruct((rows, chunks * HD), bf16),
+        ],
         scratch_shapes=[
+            pltpu.VMEM((chunks, rows, depth), bf16),
+            pltpu.VMEM((rows, span), jnp.float32),
+            pltpu.VMEM((span, HD), bf16),
+            pltpu.VMEM((span, HD), bf16),
+            pltpu.VMEM((REACH,) + key_value.shape, bf16),
             pltpu.VMEM((plane, chunks, depth, width), bf16),
             pltpu.VMEM((count, chunks, rows, depth), bf16),
             pltpu.VMEM((count, plane, rows, width), jnp.float32),
@@ -370,6 +487,9 @@
             pltpu.VMEM((count, half, rows, width), bf16),
             pltpu.VMEM((count, half, rows, width), bf16),
             pltpu.VMEM((2, 2, half, rows, width), bf16),
+            pltpu.SemaphoreType.DMA((2, REACH)),
+            pltpu.SemaphoreType.DMA((chunks,)),
+            pltpu.SemaphoreType.DMA((3, chunks)),
             pltpu.SemaphoreType.DMA((plane, chunks)),
             pltpu.SemaphoreType.DMA((2, count, chunks)),
             pltpu.SemaphoreType.DMA((count, chunks)),
@@ -378,16 +498,18 @@
             pltpu.SemaphoreType.DMA((2, 2)),
         ],
         compiler_params=pltpu.CompilerParams(
-            collective_id=1, has_side_effects=True, vmem_limit_bytes=58 * 2**20
+            collective_id=1, has_side_effects=True, vmem_limit_bytes=62 * 2**20
         ),
         cost_estimate=pl.CostEstimate(
-            flops=2 * count * plane * rows * width * chunks * depth,
-            bytes_accessed=2 * plane * width * chunks * depth,
-            transcendentals=0,
+            flops=2 * count * plane * rows * width * chunks * depth
+            + 4 * rows * span * chunks * depth,
+            bytes_accessed=2 * width * chunks * depth,
+            transcendentals=rows * span * chunks * GROUP,
         ),
-    )(attended, weights)
+    )(seg_start, cosine, sine, queries, key_value, out_weight)
     own_share = share.reshape(2 * plane, rows, width).swapaxes(0, 1).reshape(residual.shape)
-    return (residual.astype(jnp.float32) + own_share.astype(jnp.float32)).astype(bf16)
+    hidden = (residual.astype(jnp.float32) + own_share.astype(jnp.float32)).astype(bf16)
+    return hidden, key_cache
 
 
 def partner(axis, step):
@@ -509,7 +631,6 @@
     device = lax.axis_index("req")
     request_ids = jnp.arange(requests, dtype=jnp.int32)
     segments = [from_behind(segment, "req", steps) for steps in range(REACH, 0, -1)] + [segment]
-    blocks = [from_behind(key_value, "req", steps) for steps in range(REACH, 0, -1)] + [key_value]
     following = from_behind(segment, "req", -1)
     near = jnp.concatenate(segments)
     span = near.shape[0]
@@ -521,12 +642,14 @@
     cosine, sine_table = rope_tables((at - start_at).astype(jnp.float32), HD)
     cosine = jnp.concatenate([cosine, cosine], axis=1)
     sine_table = jnp.concatenate([-sine_table, sine_table], axis=1)
-    attended, key_cache = attend(
-        start_at[span - tok_rows :, None], cosine, sine_table, queries, blocks
-    )
+    own_start = start_at[span - tok_rows :, None]
     if lax.axis_size("req") == 16 and lax.axis_size("tp") == 2:
-        hidden = project_by_plane(attended, out_weight, residual)
+        hidden, key_cache = attend_and_project(
+            own_start, cosine, sine_table, queries, key_value, out_weight, residual
+        )
     else:
+        blocks = [from_behind(key_value, "req", steps) for steps in range(REACH, 0, -1)]
+        attended, key_cache = attend(own_start, cosine, sine_table, queries, blocks + [key_value])
         hidden = project_by_weights(attended, out_weight, residual)
     after = jnp.concatenate([segment[1:], following[:1]])
     final = (device == lax.axis_size("req") - 1) & (jnp.arange(tok_rows) == tok_rows - 1)

time: 391 us -> 371 us (0.949)
  Pallas kernels: 230 us -> 280 us
  waiting for transfers between devices: 28.9 us -> 0.01 us
  starting transfers between devices: 31.7 us -> 16.6 us
  between operations: 14.2 us -> 0.84 us
  local copies, waits for them, and re-layouts: 70.1 us -> 60.7 us
    pallas_call x2 -> x1, Pallas kernels: 189 us -> 241 us  [attend_and_project(): pl.pallas_call(plane_kernel, in_specs=[in_vmem] * 5 + [pl.BlockSpec(memor...]
    ppermute x9 -> x5, waiting for transfers between devices: 28.2 us -> 0.01 us  [from_behind(): lax.ppermute(value, axis, [(source, source + steps) for source in range(i...]
    all_gather x1 -> x0, local copies, waits for them, and re-layouts: 17.8 us -> none  [project_by_plane(): weights = lax.all_gather(out_weight, 'req', axis_index_groups=groups)]
    ppermute x9 -> x5, starting transfers between devices: 31.7 us -> 16.6 us  [from_behind(): lax.ppermute(value, axis, [(source, source + steps) for source in range(i...]
    unnamed x17 -> x15, local copies, waits for them, and re-layouts: 38.4 us -> 46.1 us
  transfers between devices with their start and end apart: 10 -> 5, of which waited for: 2 -> 0; matrix products, arithmetic and copies ran while one was open for 12% -> 13% of each run, Pallas kernels for 5% -> 0%
where the time goes in v3:
time: 371 us; the launch traced here: 370 us
  Pallas kernels  280 us (75%)
  local copies, waits for them, and re-layouts  60.7 us (16%)
  starting transfers between devices  16.6 us (4%)
  other arithmetic  11.5 us (3%)
    pallas_call x1, Pallas kernels, attend_and_project(): pl.pallas_call(plane_kernel, in_specs=[in_vmem] * 5 + [pl.BlockSpec(memor...  241 us
    unnamed x15, local copies, waits for them, and re-layouts  46.1 us
    pallas_call x1, Pallas kernels, finish(): pl.pallas_call(functools.partial(finish_kernel, steps_req, steps_tp), in_...  39.3 us
    ppermute x5, starting transfers between devices, from_behind(): lax.ppermute(value, axis, [(source, source + steps) for source in range(i...  16.6 us
    convert_element_type x2, local copies, waits for them, and re-layouts, attend_and_project(): own_share.astype(jnp.float32)  10.6 us
  transfers between devices with their start and end apart: 5, of which 0 were waited for; matrix products, arithmetic and copies ran while one was open for 13% of the time, Pallas kernels for 0%

profile of v3, /device:TPU:0, one launch (start us, length us, event | category | flops | bytes accessed | tf_op | source)
XLA Modules:
  0.0 369.7 jit_solution(15262660266216392011)
XLA Ops:
  0.6 1.3 collective-permute-start.4
  1.9 3.0 collective-permute-start.3
  5.0 4.8 %collective-permute-start.2 = (s32[256]{0:T(256)}, s32[256]{0:T(256)S(1)}, u32[]{:S(2)}, u32[]{:S(2)}) collective-permute-start(s32[256]{0:T(256)} %param.9), channel_id=1, source_target_pairs={{0,4},{2,6},{4,8},{6,10},{8,12},{10,14},{12,16},{14,18},{16,20},{1... | collective-permute-start | bytes 3080 | tf_op jit(solution)/shard_map/ppermute | solution.py:25
  9.8 3.9 %collective-permute-start.1 = (s32[256]{0:T(256)}, s32[256]{0:T(256)S(1)}, u32[]{:S(2)}, u32[]{:S(2)}) collective-permute-start(s32[256]{0:T(256)} %param.9), channel_id=1, source_target_pairs={{0,6},{2,8},{4,10},{6,12},{8,14},{10,16},{12,18},{14,20},{16,22},{... | collective-permute-start | bytes 3080 | tf_op jit(solution)/shard_map/ppermute | solution.py:25
  13.7 3.5 collective-permute-start
  17.3 0.8 slice.16
  18.0 0.7 broadcast_in_dim.45.gain
  18.7 5.7 %copy.25.out_weight = bf16[3584,448]{1,0:T(8,128)(2,1)} copy(bf16[3584,448]{0,1:T(8,128)(2,1)} %param.11) | data formatting | bytes 6422528 | tf_op args[4]
  24.5 39.7 %copy.29.vocab = bf16[3584,4000]{1,0:T(8,128)(2,1)} copy(bf16[3584,4000]{0,1:T(8,128)(2,1)} %param.13) | data formatting | bytes 57344000 | tf_op args[6]
  64.5 0.5 slice.17
  65.0 0.7 and_or_fusion
  65.7 0.1 fusion.2.select
  65.8 0.8 copy.24.seg_start
  66.6 2.4 fusion
  69.0 1.5 pad_maximum_fusion
  70.5 240.8 %shard_map.102 = (bf16[4,2,256,448]{3,2,1,0:T(8,128)(2,1)}, bf16[256,512]{1,0:T(8,128)(2,1)}) custom-call(s32[256,1]{1,0:T(8,128)} %copy.24.seg_start, f32[1280,128]{1,0:T(8,128)} %get-tuple-element.15.cosine, f32[1280,128]{1,0:T(8,128)} %get-tuple-element.16.sine, bf16[256,3584]{1,0:T(8,128)(2,1)} %queries.1, bf16[2,256,512]{2,1,0:T(8,128)(2,1)} %key_value.1, ...), custom_call_target="tpu_custom_call" | custom-call | flops 17850957824 | bytes 3211264 | tf_op jit(solution)/shard_map/pallas_call | solution.py:469
  311.3 4.1 %bitcast_convert_fusion = f32[8,256,448]{2,1,0:T(8,128)} fusion(bf16[4,2,256,448]{3,2,1,0:T(8,128)(2,1)} %get-tuple-element.8), kind=kLoop, calls=%fused_computation.1 | loop fusion | flops 917504 | bytes 5505024 | tf_op jit(solution)/shard_map/convert_element_type | solution.py:511
  315.4 5.3 %copy.26 = f32[8,256,448]{1,2,0:T(8,128)} copy(f32[8,256,448]{2,1,0:T(8,128)} %bitcast_convert_fusion) | data formatting | bytes 7340032 | tf_op jit(solution)/shard_map/convert_element_type | solution.py:511
  320.6 5.3 %copy.27 = f32[256,3584]{1,0:T(8,128)} copy(f32[256,3584]{0,1:T(8,128)} %bitcast.7) | data formatting | bytes 7340032 | tf_op jit(solution)/shard_map/convert_element_type | solution.py:511
  326.0 2.4 add_convert_fusion.hidden
  328.4 39.3 %shard_map.103 = (f32[8,128]{1,0:T(8,128)S(1)}, f32[8,128]{1,0:T(8,128)S(1)}) custom-call(bf16[256,8]{1,0:T(8,128)(2,1)S(1)} %fusion.2.select, bf16[256,3584]{1,0:T(8,128)(2,1)S(1)} %add_convert_fusion.hidden, bf16[1,3584]{1,0:T(2,128)(2,1)S(1)} %broadcast_in_dim.45.gain, bf16[3584,4000]{1,0:T(8,128)(2,1)} %copy.29.vocab), custom_call_target="tpu_custom_call" | custom-call | flops 229376000 | bytes 28672000 | tf_op jit(solution)/shard_map/pallas_call | solution.py:599
  367.8 0.6 slice_reduce_fusion.1
  368.4 0.6 slice_reduce_fusion
  369.0 0.7 copy.36
  (25 shorter events, 0.3 us)
Async XLA Ops:
  0.6 63.8 %collective-permute-start.4 = (s32[256]{0:T(256)}, s32[256]{0:T(256)S(1)}, u32[]{:S(2)}, u32[]{:S(2)}) collective-permute-start(s32[256]{0:T(256)} %param.9), channel_id=1, source_target_pairs={{2,0},{4,2},{6,4},{8,6},{10,8},{12,10},{14,12},{16,14},{18,16},{20... | collective-permute-start | bytes 3080 | tf_op jit(solution)/shard_map/ppermute | solution.py:25
  1.9 62.2 %collective-permute-start.3 = (s32[256]{0:T(256)}, s32[256]{0:T(256)S(1)}, u32[]{:S(2)}, u32[]{:S(2)}) collective-permute-start(s32[256]{0:T(256)} %param.9), channel_id=1, source_target_pairs={{0,2},{2,4},{4,6},{6,8},{8,10},{10,12},{12,14},{14,16},{16,18},{18... | collective-permute-start | bytes 3080 | tf_op jit(solution)/shard_map/ppermute | solution.py:25
  5.0 59.2 %collective-permute-start.2 = (s32[256]{0:T(256)}, s32[256]{0:T(256)S(1)}, u32[]{:S(2)}, u32[]{:S(2)}) collective-permute-start(s32[256]{0:T(256)} %param.9), channel_id=1, source_target_pairs={{0,4},{2,6},{4,8},{6,10},{8,12},{10,14},{12,16},{14,18},{16,20},{1... | collective-permute-start | bytes 3080 | tf_op jit(solution)/shard_map/ppermute | solution.py:25
  9.8 54.3 %collective-permute-start.1 = (s32[256]{0:T(256)}, s32[256]{0:T(256)S(1)}, u32[]{:S(2)}, u32[]{:S(2)}) collective-permute-start(s32[256]{0:T(256)} %param.9), channel_id=1, source_target_pairs={{0,6},{2,8},{4,10},{6,12},{8,14},{10,16},{12,18},{14,20},{16,22},{... | collective-permute-start | bytes 3080 | tf_op jit(solution)/shard_map/ppermute | solution.py:25
  13.7 50.4 %collective-permute-start = (s32[256]{0:T(256)}, s32[256]{0:T(256)S(1)}, u32[]{:S(2)}, u32[]{:S(2)}) collective-permute-start(s32[256]{0:T(256)} %param.9), channel_id=1, source_target_pairs={{0,8},{2,10},{4,12},{6,14},{8,16},{10,18},{12,20},{14,22},{16,24},... | collective-permute-start | bytes 3080 | tf_op jit(solution)/shard_map/ppermute | solution.py:25
  24.4 39.7 %copy-start.3 = (s32[256]{0:T(256)S(1)}, s32[256]{0:T(256)}, u32[]{:S(2)}) copy-start(s32[256]{0:T(256)} %param.9) | copy-start | bytes 3076
  320.6 5.3 %copy-start.1 = (bf16[256,3584]{1,0:T(8,128)(2,1)S(1)}, bf16[256,3584]{1,0:T(8,128)(2,1)}, u32[]{:S(2)}) copy-start(bf16[256,3584]{1,0:T(8,128)(2,1)} %param.10) | copy-start | bytes 5505028
  328.4 39.4 %copy-start = (bf16[256,3584]{1,0:T(8,128)(2,1)}, bf16[256,3584]{1,0:T(8,128)(2,1)S(1)}, u32[]{:S(2)}) copy-start(bf16[256,3584]{1,0:T(8,128)(2,1)S(1)} %add_convert_fusion.hidden) | copy-start | bytes 5505028
  328.4 40.6 %copy-start.2 = (bf16[256,512]{1,0:T(8,128)(2,1)S(1)}, bf16[256,512]{1,0:T(8,128)(2,1)}, u32[]{:S(2)}) copy-start(bf16[256,512]{1,0:T(8,128)(2,1)} %get-tuple-element.22) | copy-start | bytes 786436

commit v4 on v3

--- a/solution.py
+++ b/solution.py
@@ -126,14 +126,16 @@
 
 
 def plane_kernel(
-    seg_start, cosine, sine, queries, key_value, out_weight, share, cache,
+    seg_start, cosine, sine, queries, key_value, residual, out_weight, hidden, cache,
     attended, bias, keys, values, kv_in,
     held, blocks, acc, halves, halves_in, sums, pieces,
     kv_sems, load_sems, w_send, w_recv, z_send, z_recv, y_sems, c_send, c_recv,
 ):
     chunks, rows, depth = attended.shape
-    plane = held.shape[0]
+    plane = 4
     half = plane // 2
+    width = out_weight.shape[0]
+    wide = half * width
     count = blocks.shape[0]
     me = lax.axis_index("req")
     z, lane = me // plane, me % plane
@@ -147,10 +149,14 @@
     def at(to_z, to_y):
         return {"req": to_z * plane + lane, "tp": to_y}
 
+    def strip(c):
+        return out_weight.at[:, pl.ds(pl.multiple_of(c * depth, 128), depth)]
+
+    def slot(j, c):
+        return held.at[c, pl.ds(pl.multiple_of(j * width, 16), width), :]
+
     def load(c):
-        return pltpu.make_async_copy(
-            out_weight.at[pl.ds(c * depth, depth), :], held.at[lane, c], load_sems.at[c]
-        )
+        return pltpu.make_async_copy(strip(c), slot(lane, c), load_sems.at[c])
 
     def remote(source, landing, send, receive, target):
         return pltpu.make_async_remote_copy(
@@ -179,15 +185,15 @@
 
     def spread(kind, c):
         j = facing if kind == 2 else lane
-        source = held.at[facing, c] if kind == 2 else out_weight.at[pl.ds(c * depth, depth), :]
+        source = slot(facing, c) if kind == 2 else strip(c)
         target = facing if kind == 1 else mate
         return remote(
-            source, held.at[j, c], w_send.at[kind, c], w_recv.at[j, c], {"req": z * plane + target}
+            source, slot(j, c), w_send.at[kind, c], w_recv.at[j, c], {"req": z * plane + target}
         )
 
     def take(j, c):
         remote(
-            held.at[j, c], held.at[j, c], w_send.at[0, c], w_recv.at[j, c],
+            slot(j, c), slot(j, c), w_send.at[0, c], w_recv.at[j, c],
             {"req": z * plane + mate},
         ).wait_recv()
 
@@ -206,21 +212,24 @@
     def multiply(source, origin, c):
         rows_here = source[...]
 
-        @pl.loop(0, plane)
-        def _(j):
-            acc[origin, j] += jnp.dot(rows_here, held[j, c], preferred_element_type=jnp.float32)
+        @pl.loop(0, 2)
+        def _(i):
+            acc[origin, i] += lax.dot_general(
+                rows_here,
+                held[c, pl.ds(pl.multiple_of(i * wide, 16), wide), :],
+                (((1,), (1,)), ((), ())),
+                preferred_element_type=jnp.float32,
+            )
 
     def send_half(origin):
-        for i in range(half):
-            halves[origin, i] = acc[origin, other * half + i].astype(jnp.bfloat16)
+        halves[origin] = acc[origin, other].astype(jnp.bfloat16)
         across(origin).start()
 
     def send_home(origin):
         across(origin).wait()
-        for i in range(half):
-            sums[origin, i] = (
-                acc[origin, y * half + i] + halves_in[origin, i].astype(jnp.float32)
-            ).astype(jnp.bfloat16)
+        sums[origin] = (acc[origin, y] + halves_in[origin].astype(jnp.float32)).astype(
+            jnp.bfloat16
+        )
         stays = at_home & (origin == z)
 
         @pl.when(stays)
@@ -289,9 +298,8 @@
 
     @pl.loop(0, count)
     def _(origin):
-        @pl.loop(0, plane)
-        def _(j):
-            acc[origin, j] = jnp.zeros(acc.shape[2:], jnp.float32)
+        for i in range(2):
+            acc[origin, i] = jnp.zeros(acc.shape[2:], jnp.float32)
 
     for steps in range(1, REACH + 1):
 
@@ -349,14 +357,15 @@
         take(facing, c)
         spread(2, c).start()
 
-    @pl.loop(0, chunks)
-    def _(c):
-        load(c).wait()
-        take(mate, c)
-        take((mate + half) % plane, c)
-        multiply(attended.at[c], z, c)
-
-    send_half(z)
+    def of_blocks(step, act):
+        @pl.when(z - step >= 0)
+        def _():
+            act(z - step)
+
+        @pl.when(z + step < count)
+        def _():
+            act(z + step)
+
     for step in range(1, count):
         below, above = z - step, z + step
         from_below, from_above = below >= 0, above < count
@@ -379,41 +388,27 @@
                 def _():
                     along(blocks.at[above, c], above, c, 1).start()
 
-            @pl.when(from_below)
-            def _():
-                multiply(blocks.at[below, c], below, c)
-
-            @pl.when(from_above)
-            def _():
-                multiply(blocks.at[above, c], above, c)
-
-        @pl.when(from_below)
-        def _():
-            send_half(below)
-
-        @pl.when(from_above)
-        def _():
-            send_half(above)
+            if step == 1:
+                load(c).wait()
+                take(mate, c)
+                take((mate + half) % plane, c)
+                multiply(attended.at[c], z, c)
+            if step > 1:
+                of_blocks(step - 1, lambda origin: multiply(blocks.at[origin, c], origin, c))
+            if step == count - 1:
+                of_blocks(step, lambda origin: multiply(blocks.at[origin, c], origin, c))
 
         if step == 1:
+            send_half(z)
+        if step == 2:
+            of_blocks(1, send_half)
             send_home(z)
-        else:
-
-            @pl.when(below + 1 >= 0)
-            def _():
-                send_home(below + 1)
-
-            @pl.when(above - 1 < count)
-            def _():
-                send_home(above - 1)
-
-    @pl.when(z == count - 1)
-    def _():
-        send_home(0)
-
-    @pl.when(z == 0)
-    def _():
-        send_home(count - 1)
+        if step == 3:
+            of_blocks(2, send_half)
+            of_blocks(3, send_half)
+            of_blocks(1, send_home)
+            of_blocks(2, send_home)
+            of_blocks(3, send_home)
 
     for low in range(2):
         for side in range(2):
@@ -425,7 +420,10 @@
                     at(z, other),
                 ).wait_recv()
 
-            share[2 * low + side] = pieces[low, side]
+            columns = pl.ds((2 * low + side) * wide, wide)
+            hidden[:, columns] = (
+                residual[:, columns].astype(jnp.float32) + pieces[low, side].astype(jnp.float32)
+            ).astype(jnp.bfloat16)
 
     for steps in range(1, REACH + 1):
 
@@ -466,12 +464,12 @@
     half = plane // 2
     bf16 = jnp.bfloat16
     in_vmem = pl.BlockSpec(memory_space=pltpu.VMEM)
-    share, key_cache = pl.pallas_call(
+    hidden, key_cache = pl.pallas_call(
         plane_kernel,
-        in_specs=[in_vmem] * 5 + [pl.BlockSpec(memory_space=pl.ANY)],
+        in_specs=[in_vmem] * 6 + [pl.BlockSpec(memory_space=pl.ANY)],
         out_specs=[in_vmem, in_vmem],
         out_shape=[
-            jax.ShapeDtypeStruct((4, half, rows, width), bf16),
+            jax.ShapeDtypeStruct(residual.shape, bf16),
             jax.ShapeDtypeStruct((rows, chunks * HD), bf16),
         ],
         scratch_shapes=[
@@ -480,13 +478,13 @@
             pltpu.VMEM((span, HD), bf16),
             pltpu.VMEM((span, HD), bf16),
             pltpu.VMEM((REACH,) + key_value.shape, bf16),
-            pltpu.VMEM((plane, chunks, depth, width), bf16),
+            pltpu.VMEM((chunks, plane * width, depth), bf16),
             pltpu.VMEM((count, chunks, rows, depth), bf16),
-            pltpu.VMEM((count, plane, rows, width), jnp.float32),
-            pltpu.VMEM((count, half, rows, width), bf16),
-            pltpu.VMEM((count, half, rows, width), bf16),
-            pltpu.VMEM((count, half, rows, width), bf16),
-            pltpu.VMEM((2, 2, half, rows, width), bf16),
+            pltpu.VMEM((count, 2, rows, half * width), jnp.float32),
+            pltpu.VMEM((count, rows, half * width), bf16),
+            pltpu.VMEM((count, rows, half * width), bf16),
+            pltpu.VMEM((count, rows, half * width), bf16),
+            pltpu.VMEM((2, 2, rows, half * width), bf16),
             pltpu.SemaphoreType.DMA((2, REACH)),
             pltpu.SemaphoreType.DMA((chunks,)),
             pltpu.SemaphoreType.DMA((3, chunks)),
@@ -506,9 +504,7 @@
             bytes_accessed=2 * width * chunks * depth,
             transcendentals=rows * span * chunks * GROUP,
         ),
-    )(seg_start, cosine, sine, queries, key_value, out_weight)
-    own_share = share.reshape(2 * plane, rows, width).swapaxes(0, 1).reshape(residual.shape)
-    hidden = (residual.astype(jnp.float32) + own_share.astype(jnp.float32)).astype(bf16)
+    )(seg_start, cosine, sine, queries, key_value, residual, out_weight.T)
     return hidden, key_cache
 
 
@@ -535,7 +531,7 @@
     steps_req, steps_tp, select, hidden, gain, vocab, norm, top, weights, scaled,
     states, states_in, parts, parts_in, tops, tops_in, load_sems, sems,
 ):
-    chunks, chunk, words = weights.shape
+    chunks, chunk, depth = weights.shape
     targets = [partner("req", step) for step in range(steps_req)]
     beside = [partner("tp", step) for step in range(steps_tp)]
 
@@ -560,26 +556,26 @@
         states[step + 1] = states[step] + states_in[step]
     last_state = states[steps_req]
     scaled[...] = (last_state * gain[...].astype(jnp.float32)).astype(jnp.bfloat16)
-    edge = parts.shape[2] - 128
-    parts[0] = jnp.zeros(parts.shape[1:], jnp.float32)
-    parts[0, :, edge:] = jnp.broadcast_to(
-        jnp.sum(last_state * last_state, axis=1, keepdims=True), (parts.shape[1], 128)
+    parts[0, chunks] = jnp.broadcast_to(
+        jnp.sum(last_state * last_state, axis=1, keepdims=True), parts.shape[2:]
     )
 
     @pl.loop(0, chunks)
     def _(k):
         load(k).wait()
-        columns = pl.ds(pl.multiple_of(k * chunk, chunk), chunk)
-        parts[0, :, :words] += jnp.dot(
-            scaled[:, columns], weights[k], preferred_element_type=jnp.float32
+        parts[0, k] = lax.dot_general(
+            scaled[...],
+            weights[k],
+            (((1,), (1,)), ((), ())),
+            preferred_element_type=jnp.float32,
         )
 
     for step, target in enumerate(beside):
         exchange(parts.at[step], parts_in.at[step], sems, steps_req + step, target)
         parts[step + 1] = parts[step] + parts_in[step]
-    mean_square = parts[steps_tp, :, edge:] / D
+    mean_square = parts[steps_tp, chunks, :, :128] / D
     norm[...] = jnp.sqrt(mean_square)
-    peak = jnp.max(parts[steps_tp, :, :words], axis=1, keepdims=True)
+    peak = jnp.max(jnp.max(parts[steps_tp, :chunks], axis=0), axis=1, keepdims=True)
     tops[0] = peak * lax.rsqrt(mean_square + eps)
     for step, target in enumerate(targets):
         exchange(tops.at[step], tops_in.at[step], sems, steps_req + steps_tp + step, target)
@@ -592,8 +588,7 @@
     depth, words = vocab_weight.shape
     steps_req = lax.axis_size("req").bit_length() - 1
     steps_tp = lax.axis_size("tp").bit_length() - 1
-    chunks = 7
-    wide = -(-words // 128) * 128 + 128
+    chunks = 5 if words % 80 == 0 else 1
     in_vmem = pl.BlockSpec(memory_space=pltpu.VMEM)
     small = jax.ShapeDtypeStruct((requests, 128), jnp.float32)
     norm, top = pl.pallas_call(
@@ -602,12 +597,12 @@
         out_specs=[in_vmem, in_vmem],
         out_shape=[small, small],
         scratch_shapes=[
-            pltpu.VMEM((chunks, depth // chunks, words), jnp.bfloat16),
+            pltpu.VMEM((chunks, words // chunks, depth), jnp.bfloat16),
             pltpu.VMEM((requests, depth), jnp.bfloat16),
             pltpu.VMEM((steps_req + 1, requests, depth), jnp.float32),
             pltpu.VMEM((steps_req, requests, depth), jnp.float32),
-            pltpu.VMEM((steps_tp + 1, requests, wide), jnp.float32),
-            pltpu.VMEM((steps_tp, requests, wide), jnp.float32),
+            pltpu.VMEM((steps_tp + 1, chunks + 1, requests, words // chunks), jnp.float32),
+            pltpu.VMEM((steps_tp, chunks + 1, requests, words // chunks), jnp.float32),
             pltpu.VMEM((steps_req + 1, requests, 128), jnp.float32),
             pltpu.VMEM((steps_req, requests, 128), jnp.float32),
             pltpu.SemaphoreType.DMA((chunks,)),
@@ -621,8 +616,77 @@
             bytes_accessed=2 * depth * words,
             transcendentals=0,
         ),
-    )(select, hidden, head_gain[None, :], vocab_weight)
+    )(select, hidden, head_gain[None, :], vocab_weight.T)
     return norm[:, 0], top[:, 0]
+
+
+def near_kernel(segment, found, landing, sems):
+    me = lax.axis_index("req")
+    last = lax.axis_size("req") - 1
+    jumps = list(range(1, REACH + 1)) + [-1]
+
+    def send(number):
+        return pltpu.make_async_remote_copy(
+            src_ref=segment,
+            dst_ref=landing.at[number],
+            send_sem=sems.at[0, number],
+            recv_sem=sems.at[1, number],
+            device_id={"req": me + jumps[number]},
+            device_id_type=pl.DeviceIdType.MESH,
+        )
+
+    barrier = pltpu.get_barrier_semaphore()
+    for jump in jumps:
+
+        @pl.when((me - jump >= 0) & (me - jump <= last))
+        def _():
+            pl.semaphore_signal(
+                barrier,
+                inc=1,
+                device_id={"req": me - jump},
+                device_id_type=pl.DeviceIdType.MESH,
+            )
+
+    pl.semaphore_wait(barrier, jnp.minimum(last - me, REACH) + jnp.minimum(me, 1))
+    for number, jump in enumerate(jumps):
+
+        @pl.when((me + jump >= 0) & (me + jump <= last))
+        def _():
+            send(number).start()
+
+    for number, jump in enumerate(jumps):
+        came = (me - jump >= 0) & (me - jump <= last)
+
+        @pl.when(came)
+        def _():
+            send(number).wait_recv()
+            found[number] = landing[number]
+
+        @pl.when(jnp.logical_not(came))
+        def _():
+            found[number] = jnp.zeros(found.shape[1:], jnp.int32)
+
+    for number, jump in enumerate(jumps):
+
+        @pl.when((me + jump >= 0) & (me + jump <= last))
+        def _():
+            send(number).wait_send()
+
+
+def near_segments(segment):
+    shape = (REACH + 1, segment.shape[0] // 128, 128)
+    in_vmem = pl.BlockSpec(memory_space=pltpu.VMEM)
+    return pl.pallas_call(
+        near_kernel,
+        in_specs=[in_vmem],
+        out_specs=in_vmem,
+        out_shape=jax.ShapeDtypeStruct(shape, jnp.int32),
+        scratch_shapes=[
+            pltpu.VMEM(shape, jnp.int32),
+            pltpu.SemaphoreType.DMA((2, REACH + 1)),
+        ],
+        compiler_params=pltpu.CompilerParams(collective_id=2, has_side_effects=True),
+    )(segment.reshape(shape[1:])).reshape(REACH + 1, -1)
 
 
 def local(queries, key_value, segment, residual, out_weight, head_gain, vocab_weight):
@@ -630,8 +694,9 @@
     requests = lax.axis_size("req") // 2
     device = lax.axis_index("req")
     request_ids = jnp.arange(requests, dtype=jnp.int32)
-    segments = [from_behind(segment, "req", steps) for steps in range(REACH, 0, -1)] + [segment]
-    following = from_behind(segment, "req", -1)
+    around = near_segments(segment)
+    segments = [around[steps - 1] for steps in range(REACH, 0, -1)] + [segment]
+    following = around[REACH]
     near = jnp.concatenate(segments)
     span = near.shape[0]
     at = jnp.arange(span, dtype=jnp.int32)

time: 371 us -> 294 us (0.79)
  local copies, waits for them, and re-layouts: 60.7 us -> 11.5 us
  starting transfers between devices: 16.6 us -> 0 us
  other arithmetic: 11.5 us -> 6.29 us
  Pallas kernels: 280 us -> 275 us
    unnamed x15 -> x10, local copies, waits for them, and re-layouts: 46.1 us -> 6.14 us
    ppermute x5 -> x0, starting transfers between devices: 16.6 us -> none  [from_behind(): lax.ppermute(value, axis, [(source, source + steps) for source in range(i...]
    convert_element_type x2 -> x0, local copies, waits for them, and re-layouts: 10.6 us -> none  [attend_and_project(): own_share.astype(jnp.float32)]
    pallas_call x1 -> x2, Pallas kernels: 241 us -> 230 us  [the longest x1 225 us: attend_and_project(): pl.pallas_call(plane_kernel, in_specs=[in_vmem] * 6 + [pl.BlockSpec(memor...]
    convert_element_type x2 -> x0, other arithmetic: 6.57 us -> none  [the longest x1 4.12 us: attend_and_project(): own_share.astype(jnp.float32)]
    pallas_call x1, Pallas kernels: 39.3 us -> 44.3 us  [finish(): pl.pallas_call(functools.partial(finish_kernel, steps_req, steps_tp), in_...]
  transfers between devices with their start and end apart: 5 -> 0, of which waited for: 0 -> 0; matrix products, arithmetic and copies ran while one was open for 13% -> 0% of each run, Pallas kernels for 0% -> 0%
where the time goes in v4:
time: 294 us; the launch traced here: 293 us
  Pallas kernels  275 us (94%)
  local copies, waits for them, and re-layouts  11.5 us (4%)
  other arithmetic  6.29 us (2%)
    pallas_call x1, Pallas kernels, attend_and_project(): pl.pallas_call(plane_kernel, in_specs=[in_vmem] * 6 + [pl.BlockSpec(memor...  225 us
    pallas_call x1, Pallas kernels, finish(): pl.pallas_call(functools.partial(finish_kernel, steps_req, steps_tp), in_...  44.3 us
    unnamed x10, local copies, waits for them, and re-layouts  6.14 us

profile of v4, /device:TPU:0, one launch (start us, length us, event | category | flops | bytes accessed | tf_op | source)
XLA Modules:
  0.0 293.3 jit_solution(2147885275350713372)
XLA Ops:
  0.7 0.8 slice.40
  1.4 5.7 %shard_map.102 = s32[5,2,128]{2,1,0:T(2,128)} custom-call(s32[2,128]{1,0:T(2,128)} %bitcast.15), custom_call_target="tpu_custom_call" | custom-call | tf_op jit(solution)/shard_map/pallas_call | solution.py:679
  7.2 0.7 slice_bitcast_fusion
  7.9 0.5 slice.42
  8.4 1.4 and_or_fusion
  9.8 0.7 constant_dynamic-update-slice_fusion.4
  10.4 0.7 constant_dynamic-update-slice_fusion.3
  11.1 0.7 constant_dynamic-update-slice_fusion.2
  11.8 0.7 constant_dynamic-update-slice_fusion.1
  12.5 0.7 constant_dynamic-update-slice_fusion
  13.2 0.1 select_reduce_fusion.1
  13.3 0.1 select_reduce_fusion
  13.4 0.7 broadcast_in_dim.45.gain
  14.1 0.8 fusion.2.select
  14.9 0.8 copy.13.seg_start
  15.7 2.4 fusion
  18.1 1.5 pad_maximum_fusion
  19.6 224.7 %shard_map.103 = (bf16[256,3584]{1,0:T(8,128)(2,1)}, bf16[256,512]{1,0:T(8,128)(2,1)}) custom-call(s32[256,1]{1,0:T(8,128)} %copy.13.seg_start, f32[1280,128]{1,0:T(8,128)} %get-tuple-element.15.cosine, f32[1280,128]{1,0:T(8,128)} %get-tuple-element.16.sine, bf16[256,3584]{1,0:T(8,128)(2,1)} %queries.1, bf16[2,256,512]{2,1,0:T(8,128)(2,1)} %key_value.1, ...), custom_call_target="tpu_custom_call" | custom-call | flops 17850957824 | bytes 3211264 | tf_op jit(solution)/shard_map/pallas_call | solution.py:467
  244.3 1.5 copy-done
  245.8 44.3 %shard_map.104 = (f32[8,128]{1,0:T(8,128)S(1)}, f32[8,128]{1,0:T(8,128)S(1)}) custom-call(bf16[256,8]{1,0:T(8,128)(2,1)S(1)} %fusion.2.select, bf16[256,3584]{1,0:T(8,128)(2,1)S(1)} %copy-done, bf16[1,3584]{1,0:T(2,128)(2,1)S(1)} %broadcast_in_dim.45.gain, bf16[4000,3584]{1,0:T(8,128)(2,1)} %bitcast.14), custom_call_target="tpu_custom_call" | custom-call | flops 229376000 | bytes 28672000 | tf_op jit(solution)/shard_map/pallas_call | solution.py:594
  290.1 0.6 slice_reduce_fusion.1
  290.7 0.6 slice_reduce_fusion
  291.3 1.2 copy.22
  292.6 0.7 copy.23
  (8 shorter events, 0.0 us)
Async XLA Ops:
  244.3 1.5 copy-start
  291.3 1.2 copy-start.1
